TPU v7x, 512 devices: a whole 4x8x8 slice. The times are simulated.
512 devices in a mesh: samples: 64 (over x, z, core), targets: 8 (over y).
Axes of the slice: x: 4, y: 8, z: 8, core: 2. Of those that a mesh axis runs over, the one named last changes fastest.
Arguments:
- read_depth: bfloat16 [40960, 20480], P('samples', 'targets'), may hold values from -60 to 60, as said below
- gauss_sketch: bfloat16 [20480, 256], P('targets'), may hold values from -0.0390625 to 0.0390625
- keep_mask: int32 [20480], P('targets'), may hold values 0 or 1
Outputs:
- projection: float32 [20480, 256], P(('targets', 'samples'))
Inputs may be any that keep to these rules, and one draw needn't show every extreme that they name: `read_depth`: each entry is an independent rough value times a scale of its sample and a scale of its target.
All inputs are finite; a program needn't handle non-finite values. No bound on the sum of `keep_mask` on one device may be relied on, other than what follows from the above.
Results may differ from a plain program's by a relative error of at most 0.0012.
Values may be sent and summed in bfloat16 or wider, within the bound.
A program may use at most 64 MiB of HBM per device.

v0:
```python
import jax
import jax.numpy as jnp
from jax import lax
from jax.sharding import PartitionSpec as P


def factor_rows(sketched, gram_matrix, row_scale):
    lower = jnp.linalg.cholesky(gram_matrix)
    basis = lax.linalg.triangular_solve(
        lower, sketched, left_side=False, lower=True, transpose_a=True
    )
    return (basis / row_scale[:, None]).astype(jnp.bfloat16)


def local_gram(sketched):
    return jnp.dot(sketched.T, sketched, precision=lax.Precision.HIGHEST)


def on_device(read_depth, gauss_sketch, keep_mask):
    kept = keep_mask.astype(jnp.float32)
    masked_sketch = jnp.where(keep_mask[:, None] > 0, gauss_sketch, jnp.zeros_like(gauss_sketch))
    raw_sketch = jnp.dot(read_depth, masked_sketch, preferred_element_type=jnp.float32)
    values = read_depth.astype(jnp.float32)
    row_squares = jnp.sum(values * values * kept[None, :], axis=1)
    local_count = jnp.sum(kept)
    raw_total, square_total, kept_count = lax.psum(
        (raw_sketch, row_squares, local_count), "targets"
    )
    row_scale = jnp.sqrt((square_total + 1.0) / (kept_count + 1.0))
    sketched = raw_total / row_scale[:, None]
    gram_matrix = lax.psum(local_gram(sketched), "samples")
    weighted = factor_rows(sketched, gram_matrix, row_scale)
    term = lax.dot_general(
        read_depth, weighted, (((0,), (0,)), ((), ())), preferred_element_type=jnp.float32
    )
    return lax.psum_scatter(term * kept[:, None], "samples", scatter_dimension=0, tiled=True)


def solution(mesh):
    return jax.shard_map(
        on_device,
        mesh=mesh,
        in_specs=(P("samples", "targets"), P("targets", None), P("targets")),
        out_specs=P(("targets", "samples"), None),
        check_vma=False,
    )
```

profile of v0, /device:TPU:1, one launch (start us, length us, event | category | flops | bytes accessed | tf_op | source)
XLA Modules:
  0.0 504.0 jit_solution(13471431329510252320)
XLA Ops:
  6.5 0.7 broadcast_compare_fusion
  7.3 5.0 fusion.4
  12.4 0.6 convert_reduce_fusion
  13.0 0.9 multiply_reduce_fusion
  13.9 15.6 %all-reduce.1 = (f32[640]{0:T(1024)S(1)}, f32[]{:T(128)}) all-reduce(f32[640]{0:T(1024)S(1)} %multiply_reduce_fusion, f32[]{:T(128)} %convert_reduce_fusion), channel_id=1, replica_groups=mesh['samples'=64,'targets'=8] {'targets'}, use_global_device_ids=true, to_apply=%region_2.3 | all-reduce | flops 641 | bytes 5128 | tf_op jit(solution)/shard_map/psum | solution.py:26
  30.2 62.6 %all-reduce.5.cloned.1.call-done = f32[640,256]{0,1:T(8,128)} async-done(((f32[640,256]{0,1:T(8,128)}), f32[640,256]{0,1:T(8,128)}) %all-reduce.5.cloned.1.call-update) | async-done | bytes 655376 | tf_op jit(solution)/shard_map/psum | solution.py:26
  92.7 1.1 broadcast_divide_fusion
  93.9 1.5 fusion.22
  95.7 190.8 %all-reduce.7.cloned.1.call-done = f32[256,256]{0,1:T(8,128)} async-done(((f32[256,256]{0,1:T(8,128)}), f32[256,256]{0,1:T(8,128)}) %all-reduce.7.cloned.1.call-update) | async-done | bytes 262160 | tf_op jit(solution)/shard_map/psum | solution.py:31
  286.5 1.1 copy.8
  287.6 1.0 fusion.13
  288.6 11.7 %cholesky.50 = f32[128,128]{1,0:T(8,128)S(1)} custom-call(f32[128,128]{1,0:T(8,128)S(1)} %cholesky.118), custom_call_target="Cholesky" | custom-call | tf_op jit(solution)/shard_map/jit(cholesky)/cholesky | solution.py:8
  300.3 9.8 %custom-call.14 = f32[1,128,128]{1,2,0:T(8,128)S(1)} custom-call(f32[1,128,128]{2,1,0:T(8,128)S(1)} %get-tuple-element.28), custom_call_target="InvertDiagBlocksLowerTriangular" | custom-call | tf_op jit(solution)/shard_map/jit(cholesky)/cholesky | solution.py:8
  310.7 11.7 %cholesky.105 = f32[128,128]{1,0:T(8,128)S(1)} custom-call(f32[128,128]{1,0:T(8,128)S(1)} %convolution_subtract_fusion.1), custom_call_target="Cholesky" | custom-call | tf_op jit(solution)/shard_map/jit(cholesky)/cholesky | solution.py:8
  322.4 0.7 compare_reduce_fusion
  324.5 4.2 while.1
  324.7 0.7 fusion.32
  325.3 1.3 bitcast_dynamic-update-slice_fusion.2
  326.7 0.7 fusion.32
  327.4 1.3 bitcast_dynamic-update-slice_fusion.2
  328.7 19.7 %custom-call.15 = f32[2,128,128]{1,2,0:T(8,128)S(1)} custom-call(f32[2,128,128]{2,1,0:T(8,128)S(1)} %get-tuple-element.12), custom_call_target="InvertDiagBlocksLowerTriangular" | custom-call | tf_op jit(solution)/shard_map/triangular_solve | solution.py:9
  349.8 3.1 fusion
  352.9 2.1 copy.11
  355.1 142.4 %reduce-scatter.4.cloned.1.call-done = f32[40,256]{1,0:T(8,128)} async-done(((f32[2560,256]{1,0:T(8,128)}), f32[40,256]{1,0:T(8,128)}) %reduce-scatter.4.cloned.1.call-update) | async-done | bytes 40976 | tf_op jit(solution)/shard_map/reduce_scatter | solution.py:36
  (27 shorter events, 2.4 us)
Async XLA Ops:
  6.5 86.2 %all-reduce.5.cloned.1.call-start = ((), (), s32[]{:S(2)}) async-start(), calls=%async_computation.1 | async-start | bytes 1310720 | tf_op jit(solution)/shard_map/psum | solution.py:26
  7.2 5.1 %copy-start.1 = (s32[2560]{0:T(1024)S(1)}, s32[2560]{0:T(1024)}, u32[]{:S(2)}) copy-start(s32[2560]{0:T(1024)} %param.5) | copy-start | bytes 30724
  7.3 5.7 %copy-start = (bf16[640,2560]{1,0:T(8,128)(2,1)S(1)}, bf16[640,2560]{1,0:T(8,128)(2,1)}, u32[]{:S(2)}) copy-start(bf16[640,2560]{1,0:T(8,128)(2,1)} %param.3) | copy-start | bytes 9830404
  12.3 274.2 %all-reduce.7.cloned.1.call-start = ((), (), s32[]{:S(2)}) async-start(), calls=%async_computation.2 | async-start | bytes 524288 | tf_op jit(solution)/shard_map/psum | solution.py:31
  95.4 402.1 %reduce-scatter.4.cloned.1.call-start = ((), (), s32[]{:S(2)}) async-start(), calls=%async_computation.3 | async-start | bytes 2662400 | tf_op jit(solution)/shard_map/reduce_scatter | solution.py:36
Sparse Core Ops, SparseCore 0:
  12.4 80.2 all-reduce.4
  96.2 190.2 all-reduce.6
  355.2 142.2 reduce-scatter.3
where the time goes:
time: 509 us; the launch traced here: 504 us
  waiting for transfers between devices  396 us (78%)
  other arithmetic  58.1 us (11%)
  blocking collectives  15.6 us (3%)
  between operations  15.2 us (3%)
  matrix products  11.5 us (2%)
  local copies, waits for them, and re-layouts  7.31 us (1%)
    psum x1, waiting for transfers between devices, on_device(): gram_matrix = lax.psum(local_gram(sketched), 'samples')  191 us
    reduce_scatter x1, waiting for transfers between devices, on_device(): lax.psum_scatter(term * kept[:, None], 'samples', scatter_dimension=0, ti...  142 us
    psum x1, waiting for transfers between devices, on_device(): lax.psum((raw_sketch, row_squares, local_count), 'targets')  62.6 us
    another operation x6, other arithmetic, factor_rows(): lower = jnp.linalg.cholesky(gram_matrix)  34 us
    another operation x3, other arithmetic, factor_rows(): lax.linalg.triangular_solve(lower, sketched, left_side=False, lower=True,...  19.7 us
    psum x1, blocking collectives, on_device(): lax.psum((raw_sketch, row_squares, local_count), 'targets')  15.6 us
  transfers between devices with their start and end apart: 3, of which 3 were waited for; matrix products, arithmetic and copies ran while one was open for 0% of the time, Pallas kernels for 0%

commit v1 on v0

v1 whole, which is shorter than its diff:
```python
import functools

import jax
import jax.numpy as jnp
from jax import lax
from jax.experimental import pallas as pl
from jax.experimental.pallas import tpu as pltpu
from jax.sharding import PartitionSpec as P

MESH = pl.DeviceIdType.MESH
F32 = jnp.float32
HIGH = lax.Precision.HIGHEST
STEPS = 4
TOLERANCE = 1e-3


def far_first(n):
    return sorted(range(1, n), key=lambda d: -min(d, n - d))


def whole_max(v):
    return jnp.max(jnp.max(jnp.abs(v), axis=0, keepdims=True), axis=1, keepdims=True)


def scale_code(peak):
    return jnp.ceil(jnp.log2(jnp.maximum(peak, 1e-30)) * 256.0) + 1.0


def to_fixed(v, code):
    unit = 32767.0 * jnp.exp2(code * (-1.0 / 256.0))
    return jnp.round(v * unit).astype(jnp.int32).astype(jnp.int16)


def code_rows(code, columns):
    return jnp.broadcast_to(code.astype(jnp.int32), (16, columns)).astype(jnp.int16)


def from_fixed(message, rows):
    code = message[rows:].astype(jnp.int32).astype(F32)[0:1]
    unit = jnp.exp2(code * (1.0 / 256.0)) * (1.0 / 32767.0)
    return message[:rows].astype(jnp.int32).astype(F32) * unit


def half_lower(e):
    k = e.shape[0]
    row = lax.broadcasted_iota(jnp.int32, (k, k), 0)
    col = lax.broadcasted_iota(jnp.int32, (k, k), 1)
    return jnp.where(row > col, e, jnp.where(row == col, 0.5 * e, 0.0))


def identity(k):
    row = lax.broadcasted_iota(jnp.int32, (k, k), 0)
    col = lax.broadcasted_iota(jnp.int32, (k, k), 1)
    return jnp.where(row == col, 1.0, 0.0).astype(F32)


def times_t(a, b):
    return lax.dot_general(a, b, (((1,), (1,)), ((), ())), precision=HIGH, preferred_element_type=F32)


def times(a, b):
    return lax.dot_general(a, b, (((1,), (0,)), ((), ())), precision=HIGH, preferred_element_type=F32)


def all_bytes(ref, sem):
    return pltpu.make_async_copy(ref, ref, sem)


def main_kernel(
    NX, NY, NZ, NC,
    depth_hbm, gauss_hbm, keep_ref,
    part_ref, gram_ref, inverse_ref, off_ref,
    depth, gauss, depth_t, load_sem,
    p_send, p_recv, aux_send, aux_recv, w_all,
    g_own, gx_recv, g_sum, gz_recv, g_piece, gy_recv, g_block, g_full,
    own, c_send, c_recv, x_send, x_recv, z_send, z_recv,
    send_sem, recv_sem, core_send_sem, core_recv_sem,
):
    rows, cols = depth.shape
    K = gauss.shape[1]
    RY = rows // NY
    TS = cols // (NX * NZ * NC)
    XB = NZ * TS
    NU = NX * NC
    GX = 2 * K // NU
    GZ = GX // NZ

    s = lax.axis_index("samples")
    y = lax.axis_index("targets")
    core = lax.rem(s, NC)
    z = lax.rem(s // NC, NZ)
    x = s // (NC * NZ)
    u = x * NC + core

    def at_y(d):
        return (s, lax.rem(y + d, NY))

    def place(x1, z1, c1):
        return ((x1 * NZ + z1) * NC + c1, y)

    def at_u(d):
        u1 = lax.rem(u + d, NU)
        return place(u1 // NC, z, lax.rem(u1, NC))

    def at_z(d):
        return place(x, lax.rem(z + d, NZ), core)

    def at_x(d):
        return place(lax.rem(x + d, NX), z, core)

    def send(src, dst, phase, to):
        pltpu.make_async_remote_copy(
            src_ref=src, dst_ref=dst, send_sem=send_sem.at[phase], recv_sem=recv_sem.at[phase],
            device_id=to, device_id_type=MESH,
        ).start()

    y_order, u_order, z_order, x_order = far_first(NY), far_first(NU), far_first(NZ), far_first(NX)

    def row_block(y1):
        return pl.ds(pl.multiple_of(y1 * RY, 16), RY)

    gauss_load = pltpu.make_async_copy(gauss_hbm, gauss, load_sem.at[0])
    gauss_load.start()
    loads = []
    for i, d in enumerate(y_order + [0]):
        block = row_block(lax.rem(y + d, NY))
        load = pltpu.make_async_copy(depth_hbm.at[block], depth.at[block], load_sem.at[i + 1])
        load.start()
        loads.append(load)

    barrier = pltpu.get_barrier_semaphore()
    for d in y_order:
        pl.semaphore_signal(barrier, inc=1, device_id=at_y(d), device_id_type=MESH)
    for d in u_order:
        pl.semaphore_signal(barrier, inc=1, device_id=at_u(d), device_id_type=MESH)
    for d in z_order:
        pl.semaphore_signal(barrier, inc=1, device_id=at_z(d), device_id_type=MESH)
    pl.semaphore_wait(barrier, NY + NU + NZ - 3)

    kept = keep_ref[...].astype(F32)
    count = jnp.sum(kept, axis=1, keepdims=True)
    sub = lax.broadcasted_iota(jnp.int32, (8, 128), 0)
    gauss_load.wait()

    raw_own = None
    for i, d in enumerate(y_order + [0]):
        block = row_block(lax.rem(y + d, NY))
        loads[i].wait()
        values = depth[block, :].astype(F32) * kept
        masked = values.astype(jnp.bfloat16)
        depth[block, :] = masked
        squares = values * values
        lanes = squares[:, 0:128]
        for j in range(1, cols // 128):
            lanes = lanes + squares[:, j * 128:(j + 1) * 128]
        raw = jnp.dot(masked, gauss[...], preferred_element_type=F32)
        q_row = jnp.sum(lanes.T, axis=0, keepdims=True)
        if RY < 128:
            q_row = jnp.concatenate([q_row, jnp.zeros((1, 128 - RY), F32)], axis=1)
        if d == 0:
            raw_own = raw
            peak = jnp.zeros((1, 1), F32)
        else:
            q_col = jnp.sum(lanes, axis=1, keepdims=True)
            level = raw * lax.rsqrt(jnp.maximum(q_col, 1e-30))
            peak = scale_code(whole_max(level))
            p_send[d] = to_fixed(level, peak)
        aux = jnp.where(sub == 0, q_row, jnp.where(sub == 1, peak, jnp.where(sub == 2, count, 0.0)))
        if d == 0:
            aux_recv[0] = aux
        else:
            aux_send[d] = aux
            send(aux_send.at[d], aux_recv.at[d], 0, at_y(d))
            send(p_send.at[d], p_recv.at[d], 1, at_y(d))

    def turn(j, _):
        at = pl.ds(pl.multiple_of(j * 128, 128), 128)
        depth_t[at, :] = depth[:, at].T
        return 0

    lax.fori_loop(0, cols // 128, turn, 0)

    others = pl.ds(1, NY - 1)
    all_bytes(aux_recv.at[others], recv_sem.at[0]).wait()
    all_bytes(p_recv.at[others], recv_sem.at[1]).wait()
    q_tile = aux_recv[:, 0, :]
    q_cols = q_tile.T[:RY]
    q_total = jnp.sum(q_cols, axis=1, keepdims=True)
    counts = aux_recv[0, 2:3, 0:1]
    for d in y_order:
        counts = counts + aux_recv[d, 2:3, 0:1]
    raw = raw_own
    for d in y_order:
        unit = jnp.exp2(aux_recv[d, 1:2, 0:1] * (1.0 / 256.0)) * (1.0 / 32767.0)
        root = jnp.sqrt(jnp.maximum(q_cols[:, d:d + 1], 1e-30)) * unit
        raw = raw + p_recv[d].astype(jnp.int32).astype(F32) * root
    scale = jnp.sqrt((q_total + 1.0) / (counts + 1.0))
    sketched = raw / scale
    weighted = (sketched / scale).astype(jnp.bfloat16)

    mine = row_block(y)
    w_all[mine, :] = weighted
    for d in y_order:
        send(w_all.at[mine], w_all.at[mine], 2, at_y(d))
    gram = lax.dot_general(
        sketched.T, sketched, (((1,), (0,)), ((), ())), precision=HIGH, preferred_element_type=F32
    )
    g_own[0:K, :] = gram[:, 0:128]
    g_own[K:2 * K, :] = gram[:, 128:256]
    for d in u_order:
        u1 = lax.rem(u + d, NU)
        send(g_own.at[pl.ds(pl.multiple_of(u1 * GX, 8), GX)], gx_recv.at[d], 3, at_u(d))
    all_bytes(gx_recv.at[pl.ds(1, NU - 1)], recv_sem.at[3]).wait()
    total = g_own[pl.ds(pl.multiple_of(u * GX, 8), GX), :]
    for d in u_order:
        total = total + gx_recv[d]
    g_sum[...] = total
    for d in z_order:
        z1 = lax.rem(z + d, NZ)
        send(g_sum.at[pl.ds(pl.multiple_of(z1 * GZ, 8), GZ)], gz_recv.at[d], 4, at_z(d))
    all_bytes(gz_recv.at[pl.ds(1, NZ - 1)], recv_sem.at[4]).wait()
    piece = g_sum[pl.ds(pl.multiple_of(z * GZ, 8), GZ), :]
    for d in z_order:
        piece = piece + gz_recv[d]
    g_piece[...] = piece
    for d in y_order:
        send(g_piece, gy_recv.at[d], 5, at_y(d))

    all_bytes(w_all.at[pl.ds(0, rows - RY)], recv_sem.at[2]).wait()
    c_copies = []
    for i, d in enumerate(x_order + [0]):
        x1 = lax.rem(x + d, NX)
        big = jnp.dot(
            depth_t[pl.ds(pl.multiple_of(x1 * (XB * NC), 16), XB * NC), :], w_all[...],
            preferred_element_type=F32,
        )
        even = jnp.concatenate([big[2 * j * TS:(2 * j + 1) * TS] for j in range(NZ)], axis=0)
        odd = jnp.concatenate([big[(2 * j + 1) * TS:(2 * j + 2) * TS] for j in range(NZ)], axis=0)
        keep_half = jnp.where(core == 0, even, odd)
        give_half = jnp.where(core == 0, odd, even)
        own[d] = keep_half
        code = scale_code(whole_max(give_half))
        c_send[d, 0:XB, :] = to_fixed(give_half, code)
        c_send[d, XB:XB + 16, :] = code_rows(code, K)
        copy = pltpu.make_async_remote_copy(
            src_ref=c_send.at[d], dst_ref=c_recv.at[d],
            send_sem=core_send_sem.at[d], recv_sem=core_recv_sem.at[d],
            device_id=place(x, z, 1 - core), device_id_type=MESH,
        )
        copy.start()
        c_copies.append(copy)
        if i == 0:
            all_bytes(gy_recv.at[others], recv_sem.at[5]).wait()
            piece = g_piece[...]
            for e in y_order:
                piece = piece + gy_recv[e]
            here = pl.ds(pl.multiple_of(z * GZ, 8), GZ)
            g_block[here, :] = piece
            for e in z_order:
                send(g_block.at[here], g_block.at[here], 6, at_z(e))

    all_bytes(g_block.at[pl.ds(0, GX - GZ)], recv_sem.at[6]).wait()
    there = pl.ds(pl.multiple_of(u * GX, 8), GX)
    g_full[there, :] = g_block[...]
    for d in u_order:
        send(g_block, g_full.at[there], 7, at_u(d))

    half = None
    for i, d in enumerate(x_order + [0]):
        c_copies[i].wait()
        half = own[d] + from_fixed(c_recv[d], XB)
        if d != 0:
            code = scale_code(whole_max(half))
            x_send[d, 0:XB, :] = to_fixed(half, code)
            x_send[d, XB:XB + 16, :] = code_rows(code, K)
            send(x_send.at[d], x_recv.at[d], 8, at_x(d))
    own[0] = half

    all_bytes(g_full.at[pl.ds(0, 2 * K - GX)], recv_sem.at[7]).wait()
    gram = jnp.concatenate([g_full[0:K, :], g_full[K:2 * K, :]], axis=1)
    gram_ref[...] = gram
    eye = identity(K)
    diagonal = gram * eye
    d_row = lax.rsqrt(jnp.sum(diagonal, axis=0, keepdims=True))
    d_col = lax.rsqrt(jnp.sum(diagonal, axis=1, keepdims=True))
    unit_gram = gram * d_row * d_col
    inverse = eye - half_lower(unit_gram - eye)
    error = None
    for _ in range(STEPS):
        error = times_t(times(inverse, unit_gram), inverse) - eye
        inverse = inverse - times(half_lower(error), inverse)
    inverse_ref[...] = inverse * d_row
    off_ref[...] = jnp.broadcast_to(whole_max(error), (8, 128))

    all_bytes(x_recv.at[pl.ds(1, NX - 1)], recv_sem.at[8]).wait()
    half = own[0]
    for d in x_order:
        half = half + from_fixed(x_recv[d], XB)
    code = scale_code(whole_max(half))
    last = code_rows(code, 128)
    own[0] = half
    for d in z_order:
        z1 = lax.rem(z + d, NZ)
        v = own[0, pl.ds(pl.multiple_of(z1 * TS, 8), TS), :]
        v = jnp.concatenate([v[:, 0:128], v[:, 128:256]], axis=0)
        z_send[d, 0:2 * TS, :] = to_fixed(v, code)
        z_send[d, 2 * TS:2 * TS + 16, :] = last
        send(z_send.at[d], z_recv.at[d], 9, at_z(d))
    all_bytes(z_recv.at[pl.ds(1, NZ - 1)], recv_sem.at[9]).wait()
    v = own[0, pl.ds(pl.multiple_of(z * TS, 8), TS), :]
    v = jnp.concatenate([v[:, 0:128], v[:, 128:256]], axis=0)
    for d in z_order:
        v = v + from_fixed(z_recv[d], 2 * TS)
    part_ref[...] = jnp.concatenate([v[0:TS], v[TS:2 * TS]], axis=1)

    all_bytes(aux_send.at[others], send_sem.at[0]).wait()
    all_bytes(p_send.at[others], send_sem.at[1]).wait()
    all_bytes(w_all.at[pl.ds(0, rows - RY)], send_sem.at[2]).wait()
    all_bytes(gx_recv.at[pl.ds(1, NU - 1)], send_sem.at[3]).wait()
    all_bytes(gz_recv.at[pl.ds(1, NZ - 1)], send_sem.at[4]).wait()
    all_bytes(gy_recv.at[others], send_sem.at[5]).wait()
    all_bytes(g_block.at[pl.ds(0, GX - GZ)], send_sem.at[6]).wait()
    all_bytes(g_full.at[pl.ds(0, 2 * K - GX)], send_sem.at[7]).wait()
    all_bytes(x_send.at[pl.ds(1, NX - 1)], send_sem.at[8]).wait()
    all_bytes(z_send.at[pl.ds(1, NZ - 1)], send_sem.at[9]).wait()


def last_kernel(part_ref, inverse_ref, off_ref, gram_hbm, out_ref, work, right, sem):
    K = work.shape[0]
    settled = jnp.max(off_ref[...]) < TOLERANCE

    @pl.when(settled)
    def _():
        out_ref[...] = times_t(part_ref[...], inverse_ref[...])

    @pl.when(jnp.logical_not(settled))
    def _():
        load = pltpu.make_async_copy(gram_hbm, work, sem)
        load.start()
        load.wait()
        right[...] = identity(K)
        lane = lax.broadcasted_iota(jnp.int32, (1, K), 1)
        row = lax.broadcasted_iota(jnp.int32, (K, 1), 0)

        def step(k, _):
            m = work[...]
            top = work[pl.ds(k, 1), :]
            pivot = jnp.sum(jnp.where(lane == k, top, 0.0), axis=1, keepdims=True)
            column = jnp.sum(jnp.where(lane == k, m, 0.0), axis=1, keepdims=True)
            factor = jnp.where(row > k, column / pivot, 0.0)
            r = right[...]
            r_top = right[pl.ds(k, 1), :]
            work[...] = m - factor * top
            right[...] = r - factor * r_top
            return 0

        lax.fori_loop(0, K, step, 0)
        pivots = jnp.sum(work[...] * identity(K), axis=1, keepdims=True)
        out_ref[...] = times_t(part_ref[...], right[...] / jnp.sqrt(pivots))


def solution(mesh, sizes=(4, 8, 8, 2)):
    NX, NY, NZ, NC = sizes

    def on_device(read_depth, gauss_sketch, keep_mask):
        rows, cols = read_depth.shape
        K = gauss_sketch.shape[1]
        RY = rows // NY
        TS = cols // (NX * NZ * NC)
        XB = NZ * TS
        NU = NX * NC
        GX = 2 * K // NU
        GZ = GX // NZ
        vmem = pl.BlockSpec(memory_space=pltpu.VMEM)
        hbm = pl.BlockSpec(memory_space=pl.ANY)
        i16 = jnp.int16
        part, gram, inverse, off = pl.pallas_call(
            functools.partial(main_kernel, NX, NY, NZ, NC),
            out_shape=(
                jax.ShapeDtypeStruct((TS, K), F32),
                jax.ShapeDtypeStruct((K, K), F32),
                jax.ShapeDtypeStruct((K, K), F32),
                jax.ShapeDtypeStruct((8, 128), F32),
            ),
            in_specs=[hbm, hbm, vmem],
            out_specs=(vmem, vmem, vmem, vmem),
            scratch_shapes=[
                pltpu.VMEM((rows, cols), jnp.bfloat16),
                pltpu.VMEM((cols, K), jnp.bfloat16),
                pltpu.VMEM((cols, rows), jnp.bfloat16),
                pltpu.SemaphoreType.DMA((NY + 1,)),
                pltpu.VMEM((NY, RY, K), i16),
                pltpu.VMEM((NY, RY, K), i16),
                pltpu.VMEM((NY, 8, 128), F32),
                pltpu.VMEM((NY, 8, 128), F32),
                pltpu.VMEM((rows, K), jnp.bfloat16),
                pltpu.VMEM((2 * K, 128), F32),
                pltpu.VMEM((NU, GX, 128), F32),
                pltpu.VMEM((GX, 128), F32),
                pltpu.VMEM((NZ, GZ, 128), F32),
                pltpu.VMEM((GZ, 128), F32),
                pltpu.VMEM((NY, GZ, 128), F32),
                pltpu.VMEM((GX, 128), F32),
                pltpu.VMEM((2 * K, 128), F32),
                pltpu.VMEM((NX, XB, K), F32),
                pltpu.VMEM((NX, XB + 16, K), i16),
                pltpu.VMEM((NX, XB + 16, K), i16),
                pltpu.VMEM((NX, XB + 16, K), i16),
                pltpu.VMEM((NX, XB + 16, K), i16),
                pltpu.VMEM((NZ, 2 * TS + 16, 128), i16),
                pltpu.VMEM((NZ, 2 * TS + 16, 128), i16),
                pltpu.SemaphoreType.DMA((10,)),
                pltpu.SemaphoreType.DMA((10,)),
                pltpu.SemaphoreType.DMA((NX,)),
                pltpu.SemaphoreType.DMA((NX,)),
            ],
            compiler_params=pltpu.CompilerParams(
                collective_id=0, has_side_effects=True, vmem_limit_bytes=48 << 20
            ),
        )(read_depth, gauss_sketch, keep_mask.reshape(1, cols))
        return pl.pallas_call(
            last_kernel,
            out_shape=jax.ShapeDtypeStruct((TS, K), F32),
            in_specs=[vmem, vmem, vmem, hbm],
            out_specs=vmem,
            scratch_shapes=[
                pltpu.VMEM((K, K), F32),
                pltpu.VMEM((K, K), F32),
                pltpu.SemaphoreType.DMA,
            ],
        )(part, inverse, off, gram)

    return jax.shard_map(
        on_device,
        mesh=mesh,
        in_specs=(P("samples", "targets"), P("targets", None), P("targets")),
        out_specs=P(("targets", "samples"), None),
        check_vma=False,
    )
```

time: 509 us -> 74.2 us (0.15)
  waiting for transfers between devices: 396 us -> 0 us
  Pallas kernels: 0 us -> 66.4 us
  other arithmetic: 58.1 us -> 0 us
  blocking collectives: 15.6 us -> 0 us
  between operations: 15.2 us -> 0.03 us
  matrix products: 11.5 us -> 0 us
    psum x2 -> x0, waiting for transfers between devices: 253 us -> none  [the longest x1 191 us: on_device(): gram_matrix = lax.psum(local_gram(sketched), 'samples')]
    reduce_scatter x1 -> x0, waiting for transfers between devices: 142 us -> none  [on_device(): lax.psum_scatter(term * kept[:, None], 'samples', scatter_dimension=0, ti...]
    pallas_call x0 -> x2, Pallas kernels: none -> 66.4 us  [the longest x1 64.4 us: on_device(): pl.pallas_call(functools.partial(main_kernel, NX, NY, NZ, NC), out_shape=...]
    another operation x9 -> x0, other arithmetic: 53.7 us -> none  [the longest x6 34 us: factor_rows(): lower = jnp.linalg.cholesky(gram_matrix)]
    psum x1 -> x0, blocking collectives: 15.6 us -> none  [on_device(): lax.psum((raw_sketch, row_squares, local_count), 'targets')]
    dot_general x3 -> x0, matrix products: 9.67 us -> none  [the longest x1 5.03 us: on_device(): jnp.dot(read_depth, masked_sketch, preferred_element_type=jnp.float32)]
  transfers between devices with their start and end apart: 3 -> 0, of which waited for: 3 -> 0; matrix products, arithmetic and copies ran while one was open for 0% -> 0% of each run, Pallas kernels for 0% -> 0%
where the time goes in v1:
time: 74.2 us; the launch traced here: 73 us
  Pallas kernels  66.4 us (89%)
  local copies, waits for them, and re-layouts  6.53 us (9%)
    pallas_call x1, Pallas kernels, on_device(): pl.pallas_call(functools.partial(main_kernel, NX, NY, NZ, NC), out_shape=...  64.4 us
    unnamed x12, local copies, waits for them, and re-layouts  5.82 us
    pallas_call x1, Pallas kernels, on_device(): pl.pallas_call(last_kernel, out_shape=jax.ShapeDtypeStruct((TS, K), F32),...  2.04 us

profile of v1, /device:TPU:1, one launch (start us, length us, event | category | flops | bytes accessed | tf_op | source)
XLA Modules:
  0.0 73.0 jit_solution(13942427418072811142)
XLA Ops:
  0.0 0.7 reshape.3.keep_ref
  0.7 0.0 copy-start
  0.7 1.9 %copy-done = bf16[640,2560]{1,0:T(8,128)(2,1)S(1)} copy-done((bf16[640,2560]{1,0:T(8,128)(2,1)S(1)}, bf16[640,2560]{1,0:T(8,128)(2,1)}, u32[]{:S(2)}) %copy-start) | copy-done | bytes 3276824
  2.6 0.0 copy-start.1
  2.6 1.3 %copy-done.1 = bf16[2560,256]{1,0:T(8,128)(2,1)S(1)} copy-done((bf16[2560,256]{1,0:T(8,128)(2,1)S(1)}, bf16[2560,256]{1,0:T(8,128)(2,1)}, u32[]{:S(2)}) %copy-start.1) | copy-done | bytes 1310744
  4.0 64.4 %shard_map.37 = (f32[40,256]{1,0:T(8,128)S(1)}, f32[256,256]{1,0:T(8,128)S(1)}, f32[256,256]{1,0:T(8,128)S(1)}, f32[8,128]{1,0:T(8,128)S(1)}) custom-call(bf16[640,2560]{1,0:T(8,128)(2,1)S(1)} %copy-done, bf16[2560,256]{1,0:T(8,128)(2,1)S(1)} %copy-done.1, s32[1,2560]{1,0:T(1,128)S(1)} %reshape.3.keep_ref), custom_call_target="tpu_custom_call" | custom-call | tf_op jit(solution)/shard_map/pallas_call | solution.py:377
  68.4 0.0 copy-start.2
  68.4 0.7 copy-done.2
  69.0 0.0 copy-start.3
  69.1 0.7 copy-done.3
  69.8 0.0 copy-start.4
  69.8 0.6 copy-done.4
  70.4 0.0 copy-start.5
  70.4 0.6 copy-done.5
  70.9 2.0 %shard_map.38 = f32[40,256]{1,0:T(8,128)} custom-call(f32[40,256]{1,0:T(8,128)} %copy-done.4, f32[256,256]{1,0:T(8,128)} %copy-done.3, f32[8,128]{1,0:T(8,128)} %copy-done.5, f32[256,256]{1,0:T(8,128)} %copy-done.2), custom_call_target="tpu_custom_call" | custom-call | tf_op jit(solution)/shard_map/pallas_call | solution.py:421
Async XLA Ops:
  0.7 1.9 %copy-start = (bf16[640,2560]{1,0:T(8,128)(2,1)S(1)}, bf16[640,2560]{1,0:T(8,128)(2,1)}, u32[]{:S(2)}) copy-start(bf16[640,2560]{1,0:T(8,128)(2,1)} %depth_hbm.1) | copy-start | bytes 9830404
  2.6 1.3 %copy-start.1 = (bf16[2560,256]{1,0:T(8,128)(2,1)S(1)}, bf16[2560,256]{1,0:T(8,128)(2,1)}, u32[]{:S(2)}) copy-start(bf16[2560,256]{1,0:T(8,128)(2,1)} %gauss_hbm.1) | copy-start | bytes 3932164
  68.4 0.7 copy-start.2
  69.0 0.7 copy-start.3
  69.8 0.6 copy-start.4
  70.4 0.6 copy-start.5

commit v2 on v1

--- a/solution.py
+++ b/solution.py
@@ -10,8 +10,7 @@
 MESH = pl.DeviceIdType.MESH
 F32 = jnp.float32
 HIGH = lax.Precision.HIGHEST
-STEPS = 4
-TOLERANCE = 1e-3
+TOLERANCE = 2e-3
 
 
 def far_first(n):
@@ -54,12 +53,23 @@
     return jnp.where(row == col, 1.0, 0.0).astype(F32)
 
 
+def halves(a):
+    high = a.astype(jnp.bfloat16)
+    return high, (a - high.astype(F32)).astype(jnp.bfloat16)
+
+
+def dot(a, b, side):
+    return lax.dot_general(a, b, (((1,), (side,)), ((), ())), preferred_element_type=F32)
+
+
+def dot3(a, b, side):
+    a_high, a_low = a
+    b_high, b_low = b
+    return dot(a_high, b_high, side) + (dot(a_high, b_low, side) + dot(a_low, b_high, side))
+
+
 def times_t(a, b):
     return lax.dot_general(a, b, (((1,), (1,)), ((), ())), precision=HIGH, preferred_element_type=F32)
-
-
-def times(a, b):
-    return lax.dot_general(a, b, (((1,), (0,)), ((), ())), precision=HIGH, preferred_element_type=F32)
 
 
 def all_bytes(ref, sem):
@@ -69,12 +79,12 @@
 def main_kernel(
     NX, NY, NZ, NC,
     depth_hbm, gauss_hbm, keep_ref,
-    part_ref, gram_ref, inverse_ref, off_ref,
+    out_ref, part_ref, gram_hbm, off_ref,
     depth, gauss, depth_t, load_sem,
     p_send, p_recv, aux_send, aux_recv, w_all,
-    g_own, gx_recv, g_sum, gz_recv, g_piece, gy_recv, g_block, g_full,
-    own, c_send, c_recv, x_send, x_recv, z_send, z_recv,
-    send_sem, recv_sem, core_send_sem, core_recv_sem,
+    g_own, gx_recv, g_sum, gz_recv, g_piece, gy_recv, g_block, g_full, gram,
+    own, c_send, c_recv, h_send, h_recv, x_send, x_recv, z_send, z_recv,
+    send_sem, recv_sem, core_send_sem, core_recv_sem, h_send_sem, h_recv_sem,
 ):
     rows, cols = depth.shape
     K = gauss.shape[1]
@@ -137,7 +147,7 @@
         pl.semaphore_signal(barrier, inc=1, device_id=at_z(d), device_id_type=MESH)
     pl.semaphore_wait(barrier, NY + NU + NZ - 3)
 
-    kept = keep_ref[...].astype(F32)
+    kept = keep_ref[...].astype(F32).reshape(1, cols)
     count = jnp.sum(kept, axis=1, keepdims=True)
     sub = lax.broadcasted_iota(jnp.int32, (8, 128), 0)
     gauss_load.wait()
@@ -202,11 +212,12 @@
     w_all[mine, :] = weighted
     for d in y_order:
         send(w_all.at[mine], w_all.at[mine], 2, at_y(d))
-    gram = lax.dot_general(
-        sketched.T, sketched, (((1,), (0,)), ((), ())), precision=HIGH, preferred_element_type=F32
-    )
-    g_own[0:K, :] = gram[:, 0:128]
-    g_own[K:2 * K, :] = gram[:, 128:256]
+    turned = sketched.T
+    t_high, t_low = halves(turned)
+    s_high, s_low = halves(sketched)
+    own_gram = dot3((t_high, t_low), (s_high, s_low), 0)
+    g_own[0:K, :] = own_gram[:, 0:128]
+    g_own[K:2 * K, :] = own_gram[:, 128:256]
     for d in u_order:
         u1 = lax.rem(u + d, NU)
         send(g_own.at[pl.ds(pl.multiple_of(u1 * GX, 8), GX)], gx_recv.at[d], 3, at_u(d))
@@ -249,15 +260,37 @@
         )
         copy.start()
         c_copies.append(copy)
-        if i == 0:
-            all_bytes(gy_recv.at[others], recv_sem.at[5]).wait()
-            piece = g_piece[...]
-            for e in y_order:
-                piece = piece + gy_recv[e]
-            here = pl.ds(pl.multiple_of(z * GZ, 8), GZ)
-            g_block[here, :] = piece
-            for e in z_order:
-                send(g_block.at[here], g_block.at[here], 6, at_z(e))
+
+    all_bytes(gy_recv.at[others], recv_sem.at[5]).wait()
+    piece = g_piece[...]
+    for e in y_order:
+        piece = piece + gy_recv[e]
+    here = pl.ds(pl.multiple_of(z * GZ, 8), GZ)
+    g_block[here, :] = piece
+    for e in z_order:
+        send(g_block.at[here], g_block.at[here], 6, at_z(e))
+
+    right, left = 1, NX - 1
+    H = XB // 2
+    h_copies = []
+    for i, d in enumerate(x_order + [0]):
+        c_copies[i].wait()
+        half = own[d] + from_fixed(c_recv[d], XB)
+        if i > 0:
+            own[d] = half
+            continue
+        code = scale_code(whole_max(half))
+        fixed = to_fixed(half, code)
+        for slot, to in ((0, right), (1, left)):
+            h_send[slot, 0:H, :] = fixed[slot * H:(slot + 1) * H]
+            h_send[slot, H:H + 16, :] = code_rows(code, K)
+            copy = pltpu.make_async_remote_copy(
+                src_ref=h_send.at[slot], dst_ref=h_recv.at[slot],
+                send_sem=h_send_sem.at[slot], recv_sem=h_recv_sem.at[slot],
+                device_id=at_x(to), device_id_type=MESH,
+            )
+            copy.start()
+            h_copies.append(copy)
 
     all_bytes(g_block.at[pl.ds(0, GX - GZ)], recv_sem.at[6]).wait()
     there = pl.ds(pl.multiple_of(u * GX, 8), GX)
@@ -265,37 +298,18 @@
     for d in u_order:
         send(g_block, g_full.at[there], 7, at_u(d))
 
-    half = None
-    for i, d in enumerate(x_order + [0]):
-        c_copies[i].wait()
-        half = own[d] + from_fixed(c_recv[d], XB)
-        if d != 0:
-            code = scale_code(whole_max(half))
-            x_send[d, 0:XB, :] = to_fixed(half, code)
-            x_send[d, XB:XB + 16, :] = code_rows(code, K)
-            send(x_send.at[d], x_recv.at[d], 8, at_x(d))
-    own[0] = half
-
-    all_bytes(g_full.at[pl.ds(0, 2 * K - GX)], recv_sem.at[7]).wait()
-    gram = jnp.concatenate([g_full[0:K, :], g_full[K:2 * K, :]], axis=1)
-    gram_ref[...] = gram
-    eye = identity(K)
-    diagonal = gram * eye
-    d_row = lax.rsqrt(jnp.sum(diagonal, axis=0, keepdims=True))
-    d_col = lax.rsqrt(jnp.sum(diagonal, axis=1, keepdims=True))
-    unit_gram = gram * d_row * d_col
-    inverse = eye - half_lower(unit_gram - eye)
-    error = None
-    for _ in range(STEPS):
-        error = times_t(times(inverse, unit_gram), inverse) - eye
-        inverse = inverse - times(half_lower(error), inverse)
-    inverse_ref[...] = inverse * d_row
-    off_ref[...] = jnp.broadcast_to(whole_max(error), (8, 128))
-
-    all_bytes(x_recv.at[pl.ds(1, NX - 1)], recv_sem.at[8]).wait()
-    half = own[0]
-    for d in x_order:
-        half = half + from_fixed(x_recv[d], XB)
+    for slot, to in ((0, right), (1, left)):
+        h_copies[slot].wait()
+        mid = pl.ds(slot * H, H)
+        own[to, mid, :] = own[to, mid, :] + from_fixed(h_recv[slot], H)
+        half = own[to]
+        code = scale_code(whole_max(half))
+        x_send[slot, 0:XB, :] = to_fixed(half, code)
+        x_send[slot, XB:XB + 16, :] = code_rows(code, K)
+        send(x_send.at[slot], x_recv.at[slot], 8, at_x(to))
+    all_bytes(x_recv, recv_sem.at[8]).wait()
+
+    half = own[0] + from_fixed(x_recv[0], XB) + from_fixed(x_recv[1], XB)
     code = scale_code(whole_max(half))
     last = code_rows(code, 128)
     own[0] = half
@@ -306,12 +320,40 @@
         z_send[d, 0:2 * TS, :] = to_fixed(v, code)
         z_send[d, 2 * TS:2 * TS + 16, :] = last
         send(z_send.at[d], z_recv.at[d], 9, at_z(d))
+
+    all_bytes(g_full.at[pl.ds(0, 2 * K - GX)], recv_sem.at[7]).wait()
+    gram[:, 0:128] = g_full[0:K, :]
+    gram[:, 128:256] = g_full[K:2 * K, :]
+    gram_out = pltpu.make_async_copy(gram, gram_hbm, load_sem.at[0])
+    gram_out.start()
+    matrix = gram[...]
+    eye = identity(K)
+    diagonal = matrix * eye
+    d_row = lax.rsqrt(jnp.sum(diagonal, axis=0, keepdims=True))
+    d_col = lax.rsqrt(jnp.sum(diagonal, axis=1, keepdims=True))
+    unit_gram = matrix * d_row * d_col
+    unit_halves = halves(unit_gram)
+    inverse = eye - half_lower(unit_gram - eye)
+    rough = inverse.astype(jnp.bfloat16)
+    error = dot(dot(rough, unit_halves[0], 0).astype(jnp.bfloat16), rough, 1) - eye
+    inverse = inverse - dot(half_lower(error).astype(jnp.bfloat16), rough, 0)
+    for _ in range(2):
+        both = halves(inverse)
+        error = dot3(halves(dot3(both, unit_halves, 0)), both, 1) - eye
+        inverse = inverse - dot(half_lower(error).astype(jnp.bfloat16), both[0], 0)
+    inverse = inverse * d_row
+    off_ref[...] = jnp.broadcast_to(whole_max(error), (8, 128))
+    both = halves(inverse)
+
     all_bytes(z_recv.at[pl.ds(1, NZ - 1)], recv_sem.at[9]).wait()
     v = own[0, pl.ds(pl.multiple_of(z * TS, 8), TS), :]
     v = jnp.concatenate([v[:, 0:128], v[:, 128:256]], axis=0)
     for d in z_order:
         v = v + from_fixed(z_recv[d], 2 * TS)
-    part_ref[...] = jnp.concatenate([v[0:TS], v[TS:2 * TS]], axis=1)
+    part = jnp.concatenate([v[0:TS], v[TS:2 * TS]], axis=1)
+    part_ref[...] = part
+    out_ref[...] = dot3(halves(part), both, 1)
+    gram_out.wait()
 
     all_bytes(aux_send.at[others], send_sem.at[0]).wait()
     all_bytes(p_send.at[others], send_sem.at[1]).wait()
@@ -321,21 +363,21 @@
     all_bytes(gy_recv.at[others], send_sem.at[5]).wait()
     all_bytes(g_block.at[pl.ds(0, GX - GZ)], send_sem.at[6]).wait()
     all_bytes(g_full.at[pl.ds(0, 2 * K - GX)], send_sem.at[7]).wait()
-    all_bytes(x_send.at[pl.ds(1, NX - 1)], send_sem.at[8]).wait()
+    all_bytes(x_send, send_sem.at[8]).wait()
     all_bytes(z_send.at[pl.ds(1, NZ - 1)], send_sem.at[9]).wait()
 
 
-def last_kernel(part_ref, inverse_ref, off_ref, gram_hbm, out_ref, work, right, sem):
+def last_kernel(found_ref, off_ref, part_hbm, gram_hbm, out_ref, work, right, part, sem):
     K = work.shape[0]
     settled = jnp.max(off_ref[...]) < TOLERANCE
-
-    @pl.when(settled)
-    def _():
-        out_ref[...] = times_t(part_ref[...], inverse_ref[...])
+    out_ref[...] = found_ref[...]
 
     @pl.when(jnp.logical_not(settled))
     def _():
         load = pltpu.make_async_copy(gram_hbm, work, sem)
+        load.start()
+        load.wait()
+        load = pltpu.make_async_copy(part_hbm, part, sem)
         load.start()
         load.wait()
         right[...] = identity(K)
@@ -356,7 +398,7 @@
 
         lax.fori_loop(0, K, step, 0)
         pivots = jnp.sum(work[...] * identity(K), axis=1, keepdims=True)
-        out_ref[...] = times_t(part_ref[...], right[...] / jnp.sqrt(pivots))
+        out_ref[...] = times_t(part[...], right[...] / jnp.sqrt(pivots))
 
 
 def solution(mesh, sizes=(4, 8, 8, 2)):
@@ -374,16 +416,16 @@
         vmem = pl.BlockSpec(memory_space=pltpu.VMEM)
         hbm = pl.BlockSpec(memory_space=pl.ANY)
         i16 = jnp.int16
-        part, gram, inverse, off = pl.pallas_call(
+        found, part, gram, off = pl.pallas_call(
             functools.partial(main_kernel, NX, NY, NZ, NC),
             out_shape=(
                 jax.ShapeDtypeStruct((TS, K), F32),
-                jax.ShapeDtypeStruct((K, K), F32),
+                jax.ShapeDtypeStruct((TS, K), F32),
                 jax.ShapeDtypeStruct((K, K), F32),
                 jax.ShapeDtypeStruct((8, 128), F32),
             ),
             in_specs=[hbm, hbm, vmem],
-            out_specs=(vmem, vmem, vmem, vmem),
+            out_specs=(vmem, vmem, hbm, vmem),
             scratch_shapes=[
                 pltpu.VMEM((rows, cols), jnp.bfloat16),
                 pltpu.VMEM((cols, K), jnp.bfloat16),
@@ -402,33 +444,40 @@
                 pltpu.VMEM((NY, GZ, 128), F32),
                 pltpu.VMEM((GX, 128), F32),
                 pltpu.VMEM((2 * K, 128), F32),
+                pltpu.VMEM((K, K), F32),
                 pltpu.VMEM((NX, XB, K), F32),
                 pltpu.VMEM((NX, XB + 16, K), i16),
                 pltpu.VMEM((NX, XB + 16, K), i16),
-                pltpu.VMEM((NX, XB + 16, K), i16),
-                pltpu.VMEM((NX, XB + 16, K), i16),
+                pltpu.VMEM((2, XB // 2 + 16, K), i16),
+                pltpu.VMEM((2, XB // 2 + 16, K), i16),
+                pltpu.VMEM((2, XB + 16, K), i16),
+                pltpu.VMEM((2, XB + 16, K), i16),
                 pltpu.VMEM((NZ, 2 * TS + 16, 128), i16),
                 pltpu.VMEM((NZ, 2 * TS + 16, 128), i16),
                 pltpu.SemaphoreType.DMA((10,)),
                 pltpu.SemaphoreType.DMA((10,)),
                 pltpu.SemaphoreType.DMA((NX,)),
                 pltpu.SemaphoreType.DMA((NX,)),
+                pltpu.SemaphoreType.DMA((2,)),
+                pltpu.SemaphoreType.DMA((2,)),
             ],
             compiler_params=pltpu.CompilerParams(
-                collective_id=0, has_side_effects=True, vmem_limit_bytes=48 << 20
+                collective_id=0, has_side_effects=True, vmem_limit_bytes=60 << 20
             ),
-        )(read_depth, gauss_sketch, keep_mask.reshape(1, cols))
+        )(read_depth, gauss_sketch, keep_mask)
         return pl.pallas_call(
             last_kernel,
             out_shape=jax.ShapeDtypeStruct((TS, K), F32),
-            in_specs=[vmem, vmem, vmem, hbm],
+            in_specs=[vmem, vmem, hbm, hbm],
             out_specs=vmem,
             scratch_shapes=[
                 pltpu.VMEM((K, K), F32),
                 pltpu.VMEM((K, K), F32),
+                pltpu.VMEM((TS, K), F32),
                 pltpu.SemaphoreType.DMA,
             ],
-        )(part, inverse, off, gram)
+            compiler_params=pltpu.CompilerParams(vmem_limit_bytes=60 << 20),
+        )(found, off, part, gram)
 
     return jax.shard_map(
         on_device,

time: 74.2 us -> 59.6 us (0.80)
  the two profiles are of different devices: /device:TPU:1 before, /device:TPU:8 now
where the time goes in v2:
time: 59.6 us; the launch traced here: 59.4 us
  Pallas kernels  59.4 us (100%)
    pallas_call x1, Pallas kernels, on_device(): pl.pallas_call(functools.partial(main_kernel, NX, NY, NZ, NC), out_shape=...  57.9 us
    pallas_call x1, Pallas kernels, on_device(): pl.pallas_call(last_kernel, out_shape=jax.ShapeDtypeStruct((TS, K), F32),...  1.53 us

profile of v2, /device:TPU:8, one launch (start us, length us, event | category | flops | bytes accessed | tf_op | source)
XLA Modules:
  0.0 59.4 jit_solution(258566914167133652)
XLA Ops:
  0.0 57.9 %shard_map.37 = (f32[40,256]{1,0:T(8,128)}, f32[40,256]{1,0:T(8,128)}, f32[256,256]{1,0:T(8,128)}, f32[8,128]{1,0:T(8,128)}) custom-call(bf16[640,2560]{1,0:T(8,128)(2,1)} %depth_hbm.1, bf16[2560,256]{1,0:T(8,128)(2,1)} %gauss_hbm.1, s32[2560]{0:T(1024)} %keep_ref.1), custom_call_target="tpu_custom_call" | custom-call | tf_op jit(solution)/shard_map/pallas_call | solution.py:419
  57.9 1.5 %shard_map.38 = f32[40,256]{1,0:T(8,128)} custom-call(f32[40,256]{1,0:T(8,128)} %get-tuple-element.9.found_ref, f32[8,128]{1,0:T(8,128)} %get-tuple-element.10.off_ref, f32[40,256]{1,0:T(8,128)} %get-tuple-element.11.part_hbm, f32[256,256]{1,0:T(8,128)} %get-tuple-element.12.gram_hbm), custom_call_target="tpu_custom_call" | custom-call | tf_op jit(solution)/shard_map/pallas_call | solution.py:468

commit v3 on v2

--- a/solution.py
+++ b/solution.py
@@ -11,6 +11,8 @@
 F32 = jnp.float32
 HIGH = lax.Precision.HIGHEST
 TOLERANCE = 2e-3
+HALF = 128
+AUX, SKETCH, ROWS, G_X, G_Z, G_Y, G_BACK_Z, G_BACK_X, G_BACK_C, SUM_X, SUM_Z, PHASES = 0, 1, 3, 5, 6, 7, 8, 9, 10, 11, 13, 15
 
 
 def far_first(n):
@@ -35,9 +37,9 @@
 
 
 def from_fixed(message, rows):
-    code = message[rows:].astype(jnp.int32).astype(F32)[0:1]
-    unit = jnp.exp2(code * (1.0 / 256.0)) * (1.0 / 32767.0)
-    return message[:rows].astype(jnp.int32).astype(F32) * unit
+    values = message.astype(jnp.int32).astype(F32)
+    unit = jnp.exp2(values[rows:rows + 1] * (1.0 / 256.0)) * (1.0 / 32767.0)
+    return values[:rows] * unit
 
 
 def half_lower(e):
@@ -91,6 +93,7 @@
     RY = rows // NY
     TS = cols // (NX * NZ * NC)
     XB = NZ * TS
+    H = XB // 2
     NU = NX * NC
     GX = 2 * K // NU
     GZ = GX // NZ
@@ -100,7 +103,7 @@
     core = lax.rem(s, NC)
     z = lax.rem(s // NC, NZ)
     x = s // (NC * NZ)
-    u = x * NC + core
+    u = core * NX + x
 
     def at_y(d):
         return (s, lax.rem(y + d, NY))
@@ -110,13 +113,16 @@
 
     def at_u(d):
         u1 = lax.rem(u + d, NU)
-        return place(u1 // NC, z, lax.rem(u1, NC))
+        return place(lax.rem(u1, NX), z, u1 // NX)
 
     def at_z(d):
         return place(x, lax.rem(z + d, NZ), core)
 
     def at_x(d):
         return place(lax.rem(x + d, NX), z, core)
+
+    def at_core():
+        return place(x, z, 1 - core)
 
     def send(src, dst, phase, to):
         pltpu.make_async_remote_copy(
@@ -125,6 +131,7 @@
         ).start()
 
     y_order, u_order, z_order, x_order = far_first(NY), far_first(NU), far_first(NZ), far_first(NX)
+    others = pl.ds(1, NY - 1)
 
     def row_block(y1):
         return pl.ds(pl.multiple_of(y1 * RY, 16), RY)
@@ -174,14 +181,18 @@
             q_col = jnp.sum(lanes, axis=1, keepdims=True)
             level = raw * lax.rsqrt(jnp.maximum(q_col, 1e-30))
             peak = scale_code(whole_max(level))
-            p_send[d] = to_fixed(level, peak)
+            fixed = to_fixed(level, peak)
+            p_send[0, d] = fixed[:, :HALF]
+            p_send[1, d] = fixed[:, HALF:]
         aux = jnp.where(sub == 0, q_row, jnp.where(sub == 1, peak, jnp.where(sub == 2, count, 0.0)))
         if d == 0:
             aux_recv[0] = aux
         else:
             aux_send[d] = aux
-            send(aux_send.at[d], aux_recv.at[d], 0, at_y(d))
-            send(p_send.at[d], p_recv.at[d], 1, at_y(d))
+            send(aux_send.at[d], aux_recv.at[d], AUX, at_y(d))
+            send(p_send.at[0, d], p_recv.at[0, d], SKETCH, at_y(d))
+    for d in y_order:
+        send(p_send.at[1, d], p_recv.at[1, d], SKETCH + 1, at_y(d))
 
     def turn(j, _):
         at = pl.ds(pl.multiple_of(j * 128, 128), 128)
@@ -190,138 +201,172 @@
 
     lax.fori_loop(0, cols // 128, turn, 0)
 
-    others = pl.ds(1, NY - 1)
-    all_bytes(aux_recv.at[others], recv_sem.at[0]).wait()
-    all_bytes(p_recv.at[others], recv_sem.at[1]).wait()
-    q_tile = aux_recv[:, 0, :]
-    q_cols = q_tile.T[:RY]
+    all_bytes(aux_recv.at[others], recv_sem.at[AUX]).wait()
+    q_cols = aux_recv[:, 0, :].T[:RY]
     q_total = jnp.sum(q_cols, axis=1, keepdims=True)
     counts = aux_recv[0, 2:3, 0:1]
     for d in y_order:
         counts = counts + aux_recv[d, 2:3, 0:1]
-    raw = raw_own
+    to_scaled = lax.rsqrt((q_total + 1.0) / (counts + 1.0))
+    roots = {}
     for d in y_order:
         unit = jnp.exp2(aux_recv[d, 1:2, 0:1] * (1.0 / 256.0)) * (1.0 / 32767.0)
-        root = jnp.sqrt(jnp.maximum(q_cols[:, d:d + 1], 1e-30)) * unit
-        raw = raw + p_recv[d].astype(jnp.int32).astype(F32) * root
-    scale = jnp.sqrt((q_total + 1.0) / (counts + 1.0))
-    sketched = raw / scale
-    weighted = (sketched / scale).astype(jnp.bfloat16)
+        roots[d] = jnp.sqrt(jnp.maximum(q_cols[:, d:d + 1], 1e-30)) * unit
 
     mine = row_block(y)
-    w_all[mine, :] = weighted
-    for d in y_order:
-        send(w_all.at[mine], w_all.at[mine], 2, at_y(d))
-    turned = sketched.T
-    t_high, t_low = halves(turned)
-    s_high, s_low = halves(sketched)
-    own_gram = dot3((t_high, t_low), (s_high, s_low), 0)
-    g_own[0:K, :] = own_gram[:, 0:128]
-    g_own[K:2 * K, :] = own_gram[:, 128:256]
+    sketched = []
+    for h in range(2):
+        all_bytes(p_recv.at[h, others], recv_sem.at[SKETCH + h]).wait()
+        raw = raw_own[:, h * HALF:(h + 1) * HALF]
+        for d in y_order:
+            raw = raw + p_recv[h, d].astype(jnp.int32).astype(F32) * roots[d]
+        scaled = raw * to_scaled
+        sketched.append(scaled)
+        w_all[h, mine, :] = (scaled * to_scaled).astype(jnp.bfloat16)
+        for d in y_order:
+            send(w_all.at[h, mine], w_all.at[h, mine], ROWS + h, at_y(d))
+
+    sketched = jnp.concatenate(sketched, axis=1)
+    own_gram = dot3(halves(sketched.T), halves(sketched), 0)
+    g_own[0:K, :] = own_gram[:, :HALF]
+    g_own[K:2 * K, :] = own_gram[:, HALF:]
     for d in u_order:
         u1 = lax.rem(u + d, NU)
-        send(g_own.at[pl.ds(pl.multiple_of(u1 * GX, 8), GX)], gx_recv.at[d], 3, at_u(d))
-    all_bytes(gx_recv.at[pl.ds(1, NU - 1)], recv_sem.at[3]).wait()
+        send(g_own.at[pl.ds(pl.multiple_of(u1 * GX, 8), GX)], gx_recv.at[d], G_X, at_u(d))
+    all_bytes(gx_recv.at[pl.ds(1, NU - 1)], recv_sem.at[G_X]).wait()
     total = g_own[pl.ds(pl.multiple_of(u * GX, 8), GX), :]
     for d in u_order:
         total = total + gx_recv[d]
     g_sum[...] = total
     for d in z_order:
         z1 = lax.rem(z + d, NZ)
-        send(g_sum.at[pl.ds(pl.multiple_of(z1 * GZ, 8), GZ)], gz_recv.at[d], 4, at_z(d))
-    all_bytes(gz_recv.at[pl.ds(1, NZ - 1)], recv_sem.at[4]).wait()
-    piece = g_sum[pl.ds(pl.multiple_of(z * GZ, 8), GZ), :]
-    for d in z_order:
-        piece = piece + gz_recv[d]
-    g_piece[...] = piece
-    for d in y_order:
-        send(g_piece, gy_recv.at[d], 5, at_y(d))
-
-    all_bytes(w_all.at[pl.ds(0, rows - RY)], recv_sem.at[2]).wait()
-    c_copies = []
-    for i, d in enumerate(x_order + [0]):
-        x1 = lax.rem(x + d, NX)
-        big = jnp.dot(
-            depth_t[pl.ds(pl.multiple_of(x1 * (XB * NC), 16), XB * NC), :], w_all[...],
-            preferred_element_type=F32,
+        send(g_sum.at[pl.ds(pl.multiple_of(z1 * GZ, 8), GZ)], gz_recv.at[d], G_Z, at_z(d))
+
+    def gram_along_y():
+        all_bytes(gz_recv.at[pl.ds(1, NZ - 1)], recv_sem.at[G_Z]).wait()
+        piece = g_sum[pl.ds(pl.multiple_of(z * GZ, 8), GZ), :]
+        for d in z_order:
+            piece = piece + gz_recv[d]
+        g_piece[...] = piece
+        for d in y_order:
+            send(g_piece, gy_recv.at[d], G_Y, at_y(d))
+
+    def gram_back_along_z():
+        all_bytes(gy_recv.at[others], recv_sem.at[G_Y]).wait()
+        piece = g_piece[...]
+        for d in y_order:
+            piece = piece + gy_recv[d]
+        here = pl.ds(pl.multiple_of(z * GZ, 8), GZ)
+        g_block[here, :] = piece
+        for d in z_order:
+            send(g_block.at[here], g_block.at[here], G_BACK_Z, at_z(d))
+
+    def gram_back_along_x():
+        all_bytes(g_block.at[pl.ds(0, GX - GZ)], recv_sem.at[G_BACK_Z]).wait()
+        there = pl.ds(pl.multiple_of(u * GX, 8), GX)
+        g_full[there, :] = g_block[...]
+        for d in x_order:
+            send(g_block, g_full.at[there], G_BACK_X, at_x(d))
+
+    side = pl.ds(pl.multiple_of(core * (NX * GX), 8), NX * GX)
+
+    def gram_back_to_core():
+        all_bytes(g_full.at[pl.ds(0, (NX - 1) * GX)], recv_sem.at[G_BACK_X]).wait()
+        send(g_full.at[side], g_full.at[side], G_BACK_C, at_core())
+
+    def core_copy(h, d):
+        return pltpu.make_async_remote_copy(
+            src_ref=c_send.at[h, d], dst_ref=c_recv.at[h, d],
+            send_sem=core_send_sem.at[h, d], recv_sem=core_recv_sem.at[h, d],
+            device_id=at_core(), device_id_type=MESH,
         )
-        even = jnp.concatenate([big[2 * j * TS:(2 * j + 1) * TS] for j in range(NZ)], axis=0)
-        odd = jnp.concatenate([big[(2 * j + 1) * TS:(2 * j + 2) * TS] for j in range(NZ)], axis=0)
-        keep_half = jnp.where(core == 0, even, odd)
-        give_half = jnp.where(core == 0, odd, even)
-        own[d] = keep_half
-        code = scale_code(whole_max(give_half))
-        c_send[d, 0:XB, :] = to_fixed(give_half, code)
-        c_send[d, XB:XB + 16, :] = code_rows(code, K)
-        copy = pltpu.make_async_remote_copy(
-            src_ref=c_send.at[d], dst_ref=c_recv.at[d],
-            send_sem=core_send_sem.at[d], recv_sem=core_recv_sem.at[d],
-            device_id=place(x, z, 1 - core), device_id_type=MESH,
+
+    def back_project(h):
+        all_bytes(w_all.at[h, pl.ds(0, rows - RY)], recv_sem.at[ROWS + h]).wait()
+        for d in x_order + [0]:
+            x1 = lax.rem(x + d, NX)
+            big = jnp.dot(
+                depth_t[pl.ds(pl.multiple_of(x1 * (XB * NC), 16), XB * NC), :], w_all[h],
+                preferred_element_type=F32,
+            )
+            even = jnp.concatenate([big[2 * j * TS:(2 * j + 1) * TS] for j in range(NZ)], axis=0)
+            odd = jnp.concatenate([big[(2 * j + 1) * TS:(2 * j + 2) * TS] for j in range(NZ)], axis=0)
+            give = jnp.where(core == 0, odd, even)
+            own[h, d] = jnp.where(core == 0, even, odd)
+            code = scale_code(whole_max(give))
+            c_send[h, d, 0:XB, :] = to_fixed(give, code)
+            c_send[h, d, XB:XB + 16, :] = code_rows(code, HALF)
+            core_copy(h, d).start()
+
+    ways = ((0, 1), (1, NX - 1))
+
+    def way_copy(h, slot, to):
+        return pltpu.make_async_remote_copy(
+            src_ref=h_send.at[h, slot], dst_ref=h_recv.at[h, slot],
+            send_sem=h_send_sem.at[h, slot], recv_sem=h_recv_sem.at[h, slot],
+            device_id=at_x(to), device_id_type=MESH,
         )
-        copy.start()
-        c_copies.append(copy)
-
-    all_bytes(gy_recv.at[others], recv_sem.at[5]).wait()
-    piece = g_piece[...]
-    for e in y_order:
-        piece = piece + gy_recv[e]
-    here = pl.ds(pl.multiple_of(z * GZ, 8), GZ)
-    g_block[here, :] = piece
-    for e in z_order:
-        send(g_block.at[here], g_block.at[here], 6, at_z(e))
-
-    right, left = 1, NX - 1
-    H = XB // 2
-    h_copies = []
-    for i, d in enumerate(x_order + [0]):
-        c_copies[i].wait()
-        half = own[d] + from_fixed(c_recv[d], XB)
-        if i > 0:
-            own[d] = half
-            continue
+
+    def first_along_x(h):
+        for i, d in enumerate(x_order + [0]):
+            core_copy(h, d).wait()
+            half = own[h, d] + from_fixed(c_recv[h, d], XB)
+            if i > 0:
+                own[h, d] = half
+                continue
+            code = scale_code(whole_max(half))
+            fixed = to_fixed(half, code)
+            for slot, to in ways:
+                h_send[h, slot, 0:H, :] = fixed[slot * H:(slot + 1) * H]
+                h_send[h, slot, H:H + 16, :] = code_rows(code, HALF)
+                way_copy(h, slot, to).start()
+
+    def second_along_x(h):
+        for slot, to in ways:
+            way_copy(h, slot, to).wait()
+            mid = pl.ds(slot * H, H)
+            own[h, to, mid, :] = own[h, to, mid, :] + from_fixed(h_recv[h, slot], H)
+            half = own[h, to]
+            code = scale_code(whole_max(half))
+            x_send[h, slot, 0:XB, :] = to_fixed(half, code)
+            x_send[h, slot, XB:XB + 16, :] = code_rows(code, HALF)
+            send(x_send.at[h, slot], x_recv.at[h, slot], SUM_X + h, at_x(to))
+
+    def along_z(h):
+        all_bytes(x_recv.at[h], recv_sem.at[SUM_X + h]).wait()
+        half = own[h, 0] + from_fixed(x_recv[h, 0], XB) + from_fixed(x_recv[h, 1], XB)
         code = scale_code(whole_max(half))
-        fixed = to_fixed(half, code)
-        for slot, to in ((0, right), (1, left)):
-            h_send[slot, 0:H, :] = fixed[slot * H:(slot + 1) * H]
-            h_send[slot, H:H + 16, :] = code_rows(code, K)
-            copy = pltpu.make_async_remote_copy(
-                src_ref=h_send.at[slot], dst_ref=h_recv.at[slot],
-                send_sem=h_send_sem.at[slot], recv_sem=h_recv_sem.at[slot],
-                device_id=at_x(to), device_id_type=MESH,
-            )
-            copy.start()
-            h_copies.append(copy)
-
-    all_bytes(g_block.at[pl.ds(0, GX - GZ)], recv_sem.at[6]).wait()
-    there = pl.ds(pl.multiple_of(u * GX, 8), GX)
-    g_full[there, :] = g_block[...]
-    for d in u_order:
-        send(g_block, g_full.at[there], 7, at_u(d))
-
-    for slot, to in ((0, right), (1, left)):
-        h_copies[slot].wait()
-        mid = pl.ds(slot * H, H)
-        own[to, mid, :] = own[to, mid, :] + from_fixed(h_recv[slot], H)
-        half = own[to]
-        code = scale_code(whole_max(half))
-        x_send[slot, 0:XB, :] = to_fixed(half, code)
-        x_send[slot, XB:XB + 16, :] = code_rows(code, K)
-        send(x_send.at[slot], x_recv.at[slot], 8, at_x(to))
-    all_bytes(x_recv, recv_sem.at[8]).wait()
-
-    half = own[0] + from_fixed(x_recv[0], XB) + from_fixed(x_recv[1], XB)
-    code = scale_code(whole_max(half))
-    last = code_rows(code, 128)
-    own[0] = half
-    for d in z_order:
-        z1 = lax.rem(z + d, NZ)
-        v = own[0, pl.ds(pl.multiple_of(z1 * TS, 8), TS), :]
-        v = jnp.concatenate([v[:, 0:128], v[:, 128:256]], axis=0)
-        z_send[d, 0:2 * TS, :] = to_fixed(v, code)
-        z_send[d, 2 * TS:2 * TS + 16, :] = last
-        send(z_send.at[d], z_recv.at[d], 9, at_z(d))
-
-    all_bytes(g_full.at[pl.ds(0, 2 * K - GX)], recv_sem.at[7]).wait()
+        unit = 32767.0 * jnp.exp2(code * (-1.0 / 256.0))
+        tail = jnp.broadcast_to(code, (8, HALF))
+        own[h, 0] = half
+        for d in z_order:
+            z1 = lax.rem(z + d, NZ)
+            v = own[h, 0, pl.ds(pl.multiple_of(z1 * TS, 8), TS), :]
+            v = jnp.concatenate([jnp.round(v * unit), tail], axis=0)
+            z_send[h, d] = v.astype(jnp.int32).astype(jnp.int16)
+            send(z_send.at[h, d], z_recv.at[h, d], SUM_Z + h, at_z(d))
+
+    def total_along_z(h):
+        all_bytes(z_recv.at[h, pl.ds(1, NZ - 1)], recv_sem.at[SUM_Z + h]).wait()
+        v = own[h, 0, pl.ds(pl.multiple_of(z * TS, 8), TS), :]
+        for d in z_order:
+            v = v + from_fixed(z_recv[h, d], TS)
+        return v
+
+    gram_along_y()
+    back_project(0)
+    first_along_x(0)
+    back_project(1)
+    second_along_x(0)
+    gram_back_along_z()
+    first_along_x(1)
+    gram_back_along_x()
+    along_z(0)
+    second_along_x(1)
+    gram_back_to_core()
+    along_z(1)
+
+    all_bytes(g_full.at[pl.ds(0, NX * GX)], recv_sem.at[G_BACK_C]).wait()
     gram[:, 0:128] = g_full[0:K, :]
     gram[:, 128:256] = g_full[K:2 * K, :]
     gram_out = pltpu.make_async_copy(gram, gram_hbm, load_sem.at[0])
@@ -345,26 +390,23 @@
     off_ref[...] = jnp.broadcast_to(whole_max(error), (8, 128))
     both = halves(inverse)
 
-    all_bytes(z_recv.at[pl.ds(1, NZ - 1)], recv_sem.at[9]).wait()
-    v = own[0, pl.ds(pl.multiple_of(z * TS, 8), TS), :]
-    v = jnp.concatenate([v[:, 0:128], v[:, 128:256]], axis=0)
-    for d in z_order:
-        v = v + from_fixed(z_recv[d], 2 * TS)
-    part = jnp.concatenate([v[0:TS], v[TS:2 * TS]], axis=1)
+    part = jnp.concatenate([total_along_z(0), total_along_z(1)], axis=1)
     part_ref[...] = part
     out_ref[...] = dot3(halves(part), both, 1)
     gram_out.wait()
 
-    all_bytes(aux_send.at[others], send_sem.at[0]).wait()
-    all_bytes(p_send.at[others], send_sem.at[1]).wait()
-    all_bytes(w_all.at[pl.ds(0, rows - RY)], send_sem.at[2]).wait()
-    all_bytes(gx_recv.at[pl.ds(1, NU - 1)], send_sem.at[3]).wait()
-    all_bytes(gz_recv.at[pl.ds(1, NZ - 1)], send_sem.at[4]).wait()
-    all_bytes(gy_recv.at[others], send_sem.at[5]).wait()
-    all_bytes(g_block.at[pl.ds(0, GX - GZ)], send_sem.at[6]).wait()
-    all_bytes(g_full.at[pl.ds(0, 2 * K - GX)], send_sem.at[7]).wait()
-    all_bytes(x_send, send_sem.at[8]).wait()
-    all_bytes(z_send.at[pl.ds(1, NZ - 1)], send_sem.at[9]).wait()
+    all_bytes(aux_send.at[others], send_sem.at[AUX]).wait()
+    for h in range(2):
+        all_bytes(p_send.at[h, others], send_sem.at[SKETCH + h]).wait()
+        all_bytes(w_all.at[h, pl.ds(0, rows - RY)], send_sem.at[ROWS + h]).wait()
+        all_bytes(x_send.at[h], send_sem.at[SUM_X + h]).wait()
+        all_bytes(z_send.at[h, pl.ds(1, NZ - 1)], send_sem.at[SUM_Z + h]).wait()
+    all_bytes(gx_recv.at[pl.ds(1, NU - 1)], send_sem.at[G_X]).wait()
+    all_bytes(gz_recv.at[pl.ds(1, NZ - 1)], send_sem.at[G_Z]).wait()
+    all_bytes(gy_recv.at[others], send_sem.at[G_Y]).wait()
+    all_bytes(g_block.at[pl.ds(0, GX - GZ)], send_sem.at[G_BACK_Z]).wait()
+    all_bytes(g_full.at[pl.ds(0, (NX - 1) * GX)], send_sem.at[G_BACK_X]).wait()
+    all_bytes(g_full.at[side], send_sem.at[G_BACK_C]).wait()
 
 
 def last_kernel(found_ref, off_ref, part_hbm, gram_hbm, out_ref, work, right, part, sem):
@@ -431,11 +473,11 @@
                 pltpu.VMEM((cols, K), jnp.bfloat16),
                 pltpu.VMEM((cols, rows), jnp.bfloat16),
                 pltpu.SemaphoreType.DMA((NY + 1,)),
-                pltpu.VMEM((NY, RY, K), i16),
-                pltpu.VMEM((NY, RY, K), i16),
+                pltpu.VMEM((2, NY, RY, HALF), i16),
+                pltpu.VMEM((2, NY, RY, HALF), i16),
                 pltpu.VMEM((NY, 8, 128), F32),
                 pltpu.VMEM((NY, 8, 128), F32),
-                pltpu.VMEM((rows, K), jnp.bfloat16),
+                pltpu.VMEM((2, rows, HALF), jnp.bfloat16),
                 pltpu.VMEM((2 * K, 128), F32),
                 pltpu.VMEM((NU, GX, 128), F32),
                 pltpu.VMEM((GX, 128), F32),
@@ -445,21 +487,21 @@
                 pltpu.VMEM((GX, 128), F32),
                 pltpu.VMEM((2 * K, 128), F32),
                 pltpu.VMEM((K, K), F32),
-                pltpu.VMEM((NX, XB, K), F32),
-                pltpu.VMEM((NX, XB + 16, K), i16),
-                pltpu.VMEM((NX, XB + 16, K), i16),
-                pltpu.VMEM((2, XB // 2 + 16, K), i16),
-                pltpu.VMEM((2, XB // 2 + 16, K), i16),
-                pltpu.VMEM((2, XB + 16, K), i16),
-                pltpu.VMEM((2, XB + 16, K), i16),
-                pltpu.VMEM((NZ, 2 * TS + 16, 128), i16),
-                pltpu.VMEM((NZ, 2 * TS + 16, 128), i16),
-                pltpu.SemaphoreType.DMA((10,)),
-                pltpu.SemaphoreType.DMA((10,)),
-                pltpu.SemaphoreType.DMA((NX,)),
-                pltpu.SemaphoreType.DMA((NX,)),
-                pltpu.SemaphoreType.DMA((2,)),
-                pltpu.SemaphoreType.DMA((2,)),
+                pltpu.VMEM((2, NX, XB, HALF), F32),
+                pltpu.VMEM((2, NX, XB + 16, HALF), i16),
+                pltpu.VMEM((2, NX, XB + 16, HALF), i16),
+                pltpu.VMEM((2, 2, XB // 2 + 16, HALF), i16),
+                pltpu.VMEM((2, 2, XB // 2 + 16, HALF), i16),
+                pltpu.VMEM((2, 2, XB + 16, HALF), i16),
+                pltpu.VMEM((2, 2, XB + 16, HALF), i16),
+                pltpu.VMEM((2, NZ, TS + 8, HALF), i16),
+                pltpu.VMEM((2, NZ, TS + 8, HALF), i16),
+                pltpu.SemaphoreType.DMA((PHASES,)),
+                pltpu.SemaphoreType.DMA((PHASES,)),
+                pltpu.SemaphoreType.DMA((2, NX)),
+                pltpu.SemaphoreType.DMA((2, NX)),
+                pltpu.SemaphoreType.DMA((2, 2)),
+                pltpu.SemaphoreType.DMA((2, 2)),
             ],
             compiler_params=pltpu.CompilerParams(
                 collective_id=0, has_side_effects=True, vmem_limit_bytes=60 << 20

time: 59.6 us -> 59.8 us (level)
  the two profiles are of different devices: /device:TPU:8 before, /device:TPU:1 now
where the time goes in v3:
time: 59.8 us; the launch traced here: 59 us
  Pallas kernels  59 us (99%)
    pallas_call x1, Pallas kernels, on_device(): pl.pallas_call(functools.partial(main_kernel, NX, NY, NZ, NC), out_shape=...  57.5 us
    pallas_call x1, Pallas kernels, on_device(): pl.pallas_call(last_kernel, out_shape=jax.ShapeDtypeStruct((TS, K), F32),...  1.53 us

profile of v3, /device:TPU:1, one launch (start us, length us, event | category | flops | bytes accessed | tf_op | source)
XLA Modules:
  0.0 59.0 jit_solution(8352383753294449977)
XLA Ops:
  0.0 57.5 %shard_map.37 = (f32[40,256]{1,0:T(8,128)}, f32[40,256]{1,0:T(8,128)}, f32[256,256]{1,0:T(8,128)}, f32[8,128]{1,0:T(8,128)}) custom-call(bf16[640,2560]{1,0:T(8,128)(2,1)} %depth_hbm.1, bf16[2560,256]{1,0:T(8,128)(2,1)} %gauss_hbm.1, s32[2560]{0:T(1024)} %keep_ref.1), custom_call_target="tpu_custom_call" | custom-call | tf_op jit(solution)/shard_map/pallas_call | solution.py:461
  57.5 1.5 %shard_map.38 = f32[40,256]{1,0:T(8,128)} custom-call(f32[40,256]{1,0:T(8,128)} %get-tuple-element.9.found_ref, f32[8,128]{1,0:T(8,128)} %get-tuple-element.10.off_ref, f32[40,256]{1,0:T(8,128)} %get-tuple-element.11.part_hbm, f32[256,256]{1,0:T(8,128)} %get-tuple-element.12.gram_hbm), custom_call_target="tpu_custom_call" | custom-call | tf_op jit(solution)/shard_map/pallas_call | solution.py:510

commit v4 on v3

--- a/solution.py
+++ b/solution.py
@@ -29,7 +29,7 @@
 
 def to_fixed(v, code):
     unit = 32767.0 * jnp.exp2(code * (-1.0 / 256.0))
-    return jnp.round(v * unit).astype(jnp.int32).astype(jnp.int16)
+    return (v * unit).astype(jnp.int32).astype(jnp.int16)
 
 
 def code_rows(code, columns):
@@ -82,10 +82,10 @@
     NX, NY, NZ, NC,
     depth_hbm, gauss_hbm, keep_ref,
     out_ref, part_ref, gram_hbm, off_ref,
-    depth, gauss, depth_t, load_sem,
+    depth, gauss, keep_col, depth_t, load_sem,
     p_send, p_recv, aux_send, aux_recv, w_all,
     g_own, gx_recv, g_sum, gz_recv, g_piece, gy_recv, g_block, g_full, gram,
-    own, c_send, c_recv, h_send, h_recv, x_send, x_recv, z_send, z_recv,
+    terms, c_recv, own, h_send, h_recv, x_send, x_recv, z_send, z_recv,
     send_sem, recv_sem, core_send_sem, core_recv_sem, h_send_sem, h_recv_sem,
 ):
     rows, cols = depth.shape
@@ -136,12 +136,14 @@
     def row_block(y1):
         return pl.ds(pl.multiple_of(y1 * RY, 16), RY)
 
+    order = y_order + [0]
     gauss_load = pltpu.make_async_copy(gauss_hbm, gauss, load_sem.at[0])
     gauss_load.start()
     loads = []
-    for i, d in enumerate(y_order + [0]):
-        block = row_block(lax.rem(y + d, NY))
-        load = pltpu.make_async_copy(depth_hbm.at[block], depth.at[block], load_sem.at[i + 1])
+    for i, d in enumerate(order):
+        load = pltpu.make_async_copy(
+            depth_hbm.at[row_block(lax.rem(y + d, NY))], depth.at[pl.ds(i * RY, RY)], load_sem.at[i + 1]
+        )
         load.start()
         loads.append(load)
 
@@ -152,51 +154,57 @@
         pl.semaphore_signal(barrier, inc=1, device_id=at_u(d), device_id_type=MESH)
     for d in z_order:
         pl.semaphore_signal(barrier, inc=1, device_id=at_z(d), device_id_type=MESH)
-    pl.semaphore_wait(barrier, NY + NU + NZ - 3)
 
     kept = keep_ref[...].astype(F32).reshape(1, cols)
     count = jnp.sum(kept, axis=1, keepdims=True)
     sub = lax.broadcasted_iota(jnp.int32, (8, 128), 0)
+    for j in range(cols // 128):
+        tile = jnp.broadcast_to(kept[:, j * 128:(j + 1) * 128], (128, 128)).T
+        keep_col[j * 128:(j + 1) * 128, :] = tile.astype(jnp.bfloat16)
     gauss_load.wait()
+    for j in range(cols // 128):
+        at = slice(j * 128, (j + 1) * 128)
+        tile = keep_col[at, :]
+        for h in range(2):
+            gauss[at, h * HALF:(h + 1) * HALF] = gauss[at, h * HALF:(h + 1) * HALF] * tile
 
     raw_own = None
-    for i, d in enumerate(y_order + [0]):
-        block = row_block(lax.rem(y + d, NY))
-        loads[i].wait()
-        values = depth[block, :].astype(F32) * kept
-        masked = values.astype(jnp.bfloat16)
-        depth[block, :] = masked
-        squares = values * values
-        lanes = squares[:, 0:128]
-        for j in range(1, cols // 128):
-            lanes = lanes + squares[:, j * 128:(j + 1) * 128]
-        raw = jnp.dot(masked, gauss[...], preferred_element_type=F32)
-        q_row = jnp.sum(lanes.T, axis=0, keepdims=True)
-        if RY < 128:
-            q_row = jnp.concatenate([q_row, jnp.zeros((1, 128 - RY), F32)], axis=1)
-        if d == 0:
-            raw_own = raw
-            peak = jnp.zeros((1, 1), F32)
-        else:
-            q_col = jnp.sum(lanes, axis=1, keepdims=True)
-            level = raw * lax.rsqrt(jnp.maximum(q_col, 1e-30))
-            peak = scale_code(whole_max(level))
-            fixed = to_fixed(level, peak)
-            p_send[0, d] = fixed[:, :HALF]
-            p_send[1, d] = fixed[:, HALF:]
-        aux = jnp.where(sub == 0, q_row, jnp.where(sub == 1, peak, jnp.where(sub == 2, count, 0.0)))
-        if d == 0:
-            aux_recv[0] = aux
-        else:
-            aux_send[d] = aux
-            send(aux_send.at[d], aux_recv.at[d], AUX, at_y(d))
-            send(p_send.at[0, d], p_recv.at[0, d], SKETCH, at_y(d))
+    group = NY // 2
+    for g in range(2):
+        for i in range(g * group, (g + 1) * group):
+            loads[i].wait()
+        values = depth[g * group * RY:(g + 1) * group * RY, :]
+        raw = jnp.dot(values, gauss[...], preferred_element_type=F32)
+        q = jnp.dot(values * values, keep_col[...], preferred_element_type=F32)
+        invert = lax.rsqrt(jnp.maximum(q, 1e-30))
+        level = [raw[:, h * HALF:(h + 1) * HALF] * invert for h in range(2)]
+        peak = scale_code(jnp.maximum(whole_max(level[0]), whole_max(level[1])))
+        fixed = [to_fixed(part, peak) for part in level]
+        if g == 0:
+            pl.semaphore_wait(barrier, NY + NU + NZ - 3)
+        for i in range(g * group, (g + 1) * group):
+            d = order[i]
+            at = slice((i - g * group) * RY, (i - g * group + 1) * RY)
+            q_row = q[at].T[0:1]
+            if RY < 128:
+                q_row = jnp.concatenate([q_row, jnp.zeros((1, 128 - RY), F32)], axis=1)
+            aux = jnp.where(sub == 0, q_row, jnp.where(sub == 1, peak, jnp.where(sub == 2, count, 0.0)))
+            if d == 0:
+                raw_own = raw[at]
+                aux_recv[0] = aux
+            else:
+                p_send[0, d] = fixed[0][at]
+                p_send[1, d] = fixed[1][at]
+                aux_send[d] = aux
+                send(aux_send.at[d], aux_recv.at[d], AUX, at_y(d))
+                send(p_send.at[0, d], p_recv.at[0, d], SKETCH, at_y(d))
     for d in y_order:
         send(p_send.at[1, d], p_recv.at[1, d], SKETCH + 1, at_y(d))
 
     def turn(j, _):
         at = pl.ds(pl.multiple_of(j * 128, 128), 128)
-        depth_t[at, :] = depth[:, at].T
+        tile = keep_col[at, :]
+        depth_t[at, :] = depth[:, at].T * jnp.concatenate([tile] * (rows // 128), axis=1)
         return 0
 
     lax.fori_loop(0, cols // 128, turn, 0)
@@ -213,7 +221,6 @@
         unit = jnp.exp2(aux_recv[d, 1:2, 0:1] * (1.0 / 256.0)) * (1.0 / 32767.0)
         roots[d] = jnp.sqrt(jnp.maximum(q_cols[:, d:d + 1], 1e-30)) * unit
 
-    mine = row_block(y)
     sketched = []
     for h in range(2):
         all_bytes(p_recv.at[h, others], recv_sem.at[SKETCH + h]).wait()
@@ -222,9 +229,9 @@
             raw = raw + p_recv[h, d].astype(jnp.int32).astype(F32) * roots[d]
         scaled = raw * to_scaled
         sketched.append(scaled)
-        w_all[h, mine, :] = (scaled * to_scaled).astype(jnp.bfloat16)
+        w_all[h, NY - 1] = (scaled * to_scaled).astype(jnp.bfloat16)
         for d in y_order:
-            send(w_all.at[h, mine], w_all.at[h, mine], ROWS + h, at_y(d))
+            send(w_all.at[h, NY - 1], w_all.at[h, order.index(NY - d)], ROWS + h, at_y(d))
 
     sketched = jnp.concatenate(sketched, axis=1)
     own_gram = dot3(halves(sketched.T), halves(sketched), 0)
@@ -276,26 +283,19 @@
 
     def core_copy(h, d):
         return pltpu.make_async_remote_copy(
-            src_ref=c_send.at[h, d], dst_ref=c_recv.at[h, d],
+            src_ref=terms.at[h, d, :, 1 - core], dst_ref=c_recv.at[h, d],
             send_sem=core_send_sem.at[h, d], recv_sem=core_recv_sem.at[h, d],
             device_id=at_core(), device_id_type=MESH,
         )
 
     def back_project(h):
-        all_bytes(w_all.at[h, pl.ds(0, rows - RY)], recv_sem.at[ROWS + h]).wait()
+        all_bytes(w_all.at[h, pl.ds(0, NY - 1)], recv_sem.at[ROWS + h]).wait()
+        weights = w_all[h].reshape(rows, HALF)
         for d in x_order + [0]:
             x1 = lax.rem(x + d, NX)
-            big = jnp.dot(
-                depth_t[pl.ds(pl.multiple_of(x1 * (XB * NC), 16), XB * NC), :], w_all[h],
-                preferred_element_type=F32,
-            )
-            even = jnp.concatenate([big[2 * j * TS:(2 * j + 1) * TS] for j in range(NZ)], axis=0)
-            odd = jnp.concatenate([big[(2 * j + 1) * TS:(2 * j + 2) * TS] for j in range(NZ)], axis=0)
-            give = jnp.where(core == 0, odd, even)
-            own[h, d] = jnp.where(core == 0, even, odd)
-            code = scale_code(whole_max(give))
-            c_send[h, d, 0:XB, :] = to_fixed(give, code)
-            c_send[h, d, XB:XB + 16, :] = code_rows(code, HALF)
+            block = depth_t[pl.ds(pl.multiple_of(x1 * (XB * NC), 16), XB * NC), :]
+            product = jnp.dot(block, weights, preferred_element_type=F32)
+            terms[h, d] = product.reshape(NZ, NC, TS, HALF)
             core_copy(h, d).start()
 
     ways = ((0, 1), (1, NX - 1))
@@ -310,7 +310,7 @@
     def first_along_x(h):
         for i, d in enumerate(x_order + [0]):
             core_copy(h, d).wait()
-            half = own[h, d] + from_fixed(c_recv[h, d], XB)
+            half = (terms[h, d, :, core] + c_recv[h, d]).reshape(XB, HALF)
             if i > 0:
                 own[h, d] = half
                 continue
@@ -342,7 +342,7 @@
         for d in z_order:
             z1 = lax.rem(z + d, NZ)
             v = own[h, 0, pl.ds(pl.multiple_of(z1 * TS, 8), TS), :]
-            v = jnp.concatenate([jnp.round(v * unit), tail], axis=0)
+            v = jnp.concatenate([v * unit, tail], axis=0)
             z_send[h, d] = v.astype(jnp.int32).astype(jnp.int16)
             send(z_send.at[h, d], z_recv.at[h, d], SUM_Z + h, at_z(d))
 
@@ -398,7 +398,7 @@
     all_bytes(aux_send.at[others], send_sem.at[AUX]).wait()
     for h in range(2):
         all_bytes(p_send.at[h, others], send_sem.at[SKETCH + h]).wait()
-        all_bytes(w_all.at[h, pl.ds(0, rows - RY)], send_sem.at[ROWS + h]).wait()
+        all_bytes(w_all.at[h, pl.ds(0, NY - 1)], send_sem.at[ROWS + h]).wait()
         all_bytes(x_send.at[h], send_sem.at[SUM_X + h]).wait()
         all_bytes(z_send.at[h, pl.ds(1, NZ - 1)], send_sem.at[SUM_Z + h]).wait()
     all_bytes(gx_recv.at[pl.ds(1, NU - 1)], send_sem.at[G_X]).wait()
@@ -471,13 +471,14 @@
             scratch_shapes=[
                 pltpu.VMEM((rows, cols), jnp.bfloat16),
                 pltpu.VMEM((cols, K), jnp.bfloat16),
+                pltpu.VMEM((cols, 128), jnp.bfloat16),
                 pltpu.VMEM((cols, rows), jnp.bfloat16),
                 pltpu.SemaphoreType.DMA((NY + 1,)),
                 pltpu.VMEM((2, NY, RY, HALF), i16),
                 pltpu.VMEM((2, NY, RY, HALF), i16),
                 pltpu.VMEM((NY, 8, 128), F32),
                 pltpu.VMEM((NY, 8, 128), F32),
-                pltpu.VMEM((2, rows, HALF), jnp.bfloat16),
+                pltpu.VMEM((2, NY, RY, HALF), jnp.bfloat16),
                 pltpu.VMEM((2 * K, 128), F32),
                 pltpu.VMEM((NU, GX, 128), F32),
                 pltpu.VMEM((GX, 128), F32),
@@ -487,9 +488,9 @@
                 pltpu.VMEM((GX, 128), F32),
                 pltpu.VMEM((2 * K, 128), F32),
                 pltpu.VMEM((K, K), F32),
+                pltpu.VMEM((2, NX, NZ, NC, TS, HALF), F32),
+                pltpu.VMEM((2, NX, NZ, TS, HALF), F32),
                 pltpu.VMEM((2, NX, XB, HALF), F32),
-                pltpu.VMEM((2, NX, XB + 16, HALF), i16),
-                pltpu.VMEM((2, NX, XB + 16, HALF), i16),
                 pltpu.VMEM((2, 2, XB // 2 + 16, HALF), i16),
                 pltpu.VMEM((2, 2, XB // 2 + 16, HALF), i16),
                 pltpu.VMEM((2, 2, XB + 16, HALF), i16),

time: 59.8 us -> 58.1 us (0.972)
  Pallas kernels: 59 us -> 57.8 us
    pallas_call x1, Pallas kernels: 57.5 us -> 56.3 us  [on_device(): pl.pallas_call(functools.partial(main_kernel, NX, NY, NZ, NC), out_shape=...]
where the time goes in v4:
time: 58.1 us; the launch traced here: 57.9 us
  Pallas kernels  57.8 us (99%)
    pallas_call x1, Pallas kernels, on_device(): pl.pallas_call(functools.partial(main_kernel, NX, NY, NZ, NC), out_shape=...  56.3 us
    pallas_call x1, Pallas kernels, on_device(): pl.pallas_call(last_kernel, out_shape=jax.ShapeDtypeStruct((TS, K), F32),...  1.53 us

profile of v4, /device:TPU:1, one launch (start us, length us, event | category | flops | bytes accessed | tf_op | source)
XLA Modules:
  0.0 57.9 jit_solution(13163748323132008696)
XLA Ops:
  0.0 56.3 %shard_map.37 = (f32[40,256]{1,0:T(8,128)}, f32[40,256]{1,0:T(8,128)}, f32[256,256]{1,0:T(8,128)}, f32[8,128]{1,0:T(8,128)}) custom-call(bf16[640,2560]{1,0:T(8,128)(2,1)} %depth_hbm.1, bf16[2560,256]{1,0:T(8,128)(2,1)} %gauss_hbm.1, s32[2560]{0:T(1024)} %keep_ref.1), custom_call_target="tpu_custom_call" | custom-call | tf_op jit(solution)/shard_map/pallas_call | solution.py:461
  56.3 1.5 %shard_map.38 = f32[40,256]{1,0:T(8,128)} custom-call(f32[40,256]{1,0:T(8,128)} %get-tuple-element.9.found_ref, f32[8,128]{1,0:T(8,128)} %get-tuple-element.10.off_ref, f32[40,256]{1,0:T(8,128)} %get-tuple-element.11.part_hbm, f32[256,256]{1,0:T(8,128)} %get-tuple-element.12.gram_hbm), custom_call_target="tpu_custom_call" | custom-call | tf_op jit(solution)/shard_map/pallas_call | solution.py:511

commit v5 on v4

--- a/solution.py
+++ b/solution.py
@@ -12,7 +12,9 @@
 HIGH = lax.Precision.HIGHEST
 TOLERANCE = 2e-3
 HALF = 128
-AUX, SKETCH, ROWS, G_X, G_Z, G_Y, G_BACK_Z, G_BACK_X, G_BACK_C, SUM_X, SUM_Z, PHASES = 0, 1, 3, 5, 6, 7, 8, 9, 10, 11, 13, 15
+AUX_FAR, SKETCH_FAR, AUX, SKETCH, G_X, G_Z, G_Y, G_BACK_Z, G_BACK_X, G_BACK_C = 0, 1, 2, 3, 5, 6, 7, 8, 9, 10
+SUM_X, SUM_Z, ROWS_NEAR, ROWS_UP, ROWS_DOWN, ROWS_FAR, PHASES = 11, 13, 15, 17, 19, 21, 23
+CUT = 48
 
 
 def far_first(n):
@@ -83,7 +85,7 @@
     depth_hbm, gauss_hbm, keep_ref,
     out_ref, part_ref, gram_hbm, off_ref,
     depth, gauss, keep_col, depth_t, load_sem,
-    p_send, p_recv, aux_send, aux_recv, w_all,
+    f_send, f_recv, fx_send, fx_recv, p_send, p_recv, aux_send, aux_recv, w_all,
     g_own, gx_recv, g_sum, gz_recv, g_piece, gy_recv, g_block, g_full, gram,
     terms, c_recv, own, h_send, h_recv, x_send, x_recv, z_send, z_recv,
     send_sem, recv_sem, core_send_sem, core_recv_sem, h_send_sem, h_recv_sem,
@@ -168,70 +170,138 @@
         for h in range(2):
             gauss[at, h * HALF:(h + 1) * HALF] = gauss[at, h * HALF:(h + 1) * HALF] * tile
 
-    raw_own = None
+    def aux_of(q_row, code, number):
+        return jnp.where(sub == 0, q_row, jnp.where(sub == 1, code, jnp.where(sub == 2, number, 0.0)))
+
+    def row_of(q):
+        row = q.T[0:1]
+        if RY < 128:
+            row = jnp.concatenate([row, jnp.zeros((1, 128 - RY), F32)], axis=1)
+        return row
+
+    def unit_of(aux):
+        return jnp.exp2(aux[1:2, 0:1] * (1.0 / 256.0)) * (1.0 / 32767.0)
+
+    def columns_of(tiles):
+        tile = jnp.concatenate([t[0:1] for t in tiles] + [jnp.zeros((8 - len(tiles), 128), F32)], axis=0)
+        turned = tile.T[:RY]
+        return [turned[:, i:i + 1] for i in range(len(tiles))]
+
+    def safe_root(q):
+        return jnp.sqrt(jnp.maximum(q, 1e-30))
+
+    def turn(j, _):
+        at = pl.ds(pl.multiple_of(j * 128, 128), 128)
+        tile = keep_col[at, :]
+        depth_t[at, :] = depth[:, at].T * jnp.concatenate([tile] * (rows // 128), axis=1)
+        return 0
+
     group = NY // 2
+    raws, q_rows, q_cols = {}, {}, {}
     for g in range(2):
         for i in range(g * group, (g + 1) * group):
             loads[i].wait()
         values = depth[g * group * RY:(g + 1) * group * RY, :]
         raw = jnp.dot(values, gauss[...], preferred_element_type=F32)
         q = jnp.dot(values * values, keep_col[...], preferred_element_type=F32)
-        invert = lax.rsqrt(jnp.maximum(q, 1e-30))
-        level = [raw[:, h * HALF:(h + 1) * HALF] * invert for h in range(2)]
-        peak = scale_code(jnp.maximum(whole_max(level[0]), whole_max(level[1])))
-        fixed = [to_fixed(part, peak) for part in level]
+        for i in range(group):
+            d = order[g * group + i]
+            at = slice(i * RY, (i + 1) * RY)
+            raws[d], q_rows[d], q_cols[d] = raw[at], row_of(q[at]), q[at, 0:1]
+        some = slice(0, 3 * RY) if g == 0 else slice(RY, 3 * RY)
+        invert = lax.rsqrt(jnp.maximum(q[some], 1e-30))
+        level = [raw[some, h * HALF:(h + 1) * HALF] * invert for h in range(2)]
+        code = scale_code(jnp.maximum(whole_max(level[0]), whole_max(level[1])))
+        fixed = [to_fixed(part, code) for part in level]
         if g == 0:
+            for i, d in enumerate((4, 3, 5)):
+                for h in range(2):
+                    f_send[i, :, h * HALF:(h + 1) * HALF] = fixed[h][i * RY:(i + 1) * RY]
+                fx_send[i] = aux_of(q_rows[d], code, count)
             pl.semaphore_wait(barrier, NY + NU + NZ - 3)
-        for i in range(g * group, (g + 1) * group):
-            d = order[i]
-            at = slice((i - g * group) * RY, (i - g * group + 1) * RY)
-            q_row = q[at].T[0:1]
-            if RY < 128:
-                q_row = jnp.concatenate([q_row, jnp.zeros((1, 128 - RY), F32)], axis=1)
-            aux = jnp.where(sub == 0, q_row, jnp.where(sub == 1, peak, jnp.where(sub == 2, count, 0.0)))
-            if d == 0:
-                raw_own = raw[at]
-                aux_recv[0] = aux
-            else:
-                p_send[0, d] = fixed[0][at]
-                p_send[1, d] = fixed[1][at]
-                aux_send[d] = aux
-                send(aux_send.at[d], aux_recv.at[d], AUX, at_y(d))
-                send(p_send.at[0, d], p_recv.at[0, d], SKETCH, at_y(d))
-    for d in y_order:
-        send(p_send.at[1, d], p_recv.at[1, d], SKETCH + 1, at_y(d))
-
-    def turn(j, _):
-        at = pl.ds(pl.multiple_of(j * 128, 128), 128)
-        tile = keep_col[at, :]
-        depth_t[at, :] = depth[:, at].T * jnp.concatenate([tile] * (rows // 128), axis=1)
-        return 0
-
-    lax.fori_loop(0, cols // 128, turn, 0)
-
-    all_bytes(aux_recv.at[others], recv_sem.at[AUX]).wait()
-    q_cols = aux_recv[:, 0, :].T[:RY]
-    q_total = jnp.sum(q_cols, axis=1, keepdims=True)
-    counts = aux_recv[0, 2:3, 0:1]
-    for d in y_order:
-        counts = counts + aux_recv[d, 2:3, 0:1]
+            upper, lower = pl.ds(0, CUT), pl.ds(CUT, RY - CUT)
+            send(fx_send.at[0], fx_recv.at[2], AUX_FAR, at_y(2))
+            send(fx_send.at[0], fx_recv.at[3], AUX_FAR, at_y(NY - 2))
+            send(f_send.at[0, upper], f_recv.at[2, upper], SKETCH_FAR, at_y(2))
+            send(f_send.at[0, lower], f_recv.at[2, lower], SKETCH_FAR, at_y(NY - 2))
+            for i, to in ((1, 1), (2, NY - 1)):
+                send(fx_send.at[i], fx_recv.at[i - 1], AUX_FAR, at_y(to))
+                send(f_send.at[i], f_recv.at[i - 1], SKETCH_FAR, at_y(to))
+        else:
+            for i, d in enumerate((1, NY - 1)):
+                for h in range(2):
+                    p_send[h, i] = fixed[h][i * RY:(i + 1) * RY]
+                aux_send[i] = aux_of(q_rows[d], code, count)
+                send(aux_send.at[i], aux_recv.at[i], AUX, at_y(d))
+                for h in range(2):
+                    send(p_send.at[h, i], p_recv.at[h, i], SKETCH + h, at_y(d))
+
+    tiles = cols // 128
+    lax.fori_loop(0, tiles // 2, turn, 0)
+
+    all_bytes(fx_recv, recv_sem.at[AUX_FAR]).wait()
+    all_bytes(f_recv, recv_sem.at[SKETCH_FAR]).wait()
+    lane = lax.broadcasted_iota(jnp.int32, (1, 128), 1)
+    far = [fx_recv[i] for i in range(4)]
+    far_cols = columns_of(far)
+    far_unit = [unit_of(t) for t in far]
+    last = f_recv[2].astype(jnp.int32).astype(F32)
+    row = lax.broadcasted_iota(jnp.int32, (RY, 1), 0)
+    for i, d in ((0, 2), (1, NY - 2)):
+        part = (row < CUT) if i == 0 else (row >= CUT)
+        q_part = (lane < CUT) if i == 0 else (lane >= CUT)
+        total = raws[d] + f_recv[i].astype(jnp.int32).astype(F32) * (safe_root(far_cols[i]) * far_unit[i])
+        total = total + last * jnp.where(part, safe_root(far_cols[2 + i]) * far_unit[2 + i], 0.0)
+        q_col = q_cols[d] + far_cols[i] + jnp.where(part, far_cols[2 + i], 0.0)
+        q_row = q_rows[d] + far[i][0:1] + jnp.where(q_part, far[2 + i][0:1], 0.0)
+        number = count + far[i][2:3, 0:1]
+        if i == 0:
+            number = number + far[2][2:3, 0:1]
+        level = total * lax.rsqrt(jnp.maximum(q_col, 1e-30))
+        code = scale_code(whole_max(level))
+        fixed = to_fixed(level, code)
+        aux_send[2 + i] = aux_of(q_row, code, number)
+        send(aux_send.at[2 + i], aux_recv.at[2 + i], AUX, at_y(d))
+        for h in range(2):
+            p_send[h, 2 + i] = fixed[:, h * HALF:(h + 1) * HALF]
+        send(p_send.at[0, 2 + i], p_recv.at[0, 2 + i], SKETCH, at_y(d))
+    for i, d in ((0, 2), (1, NY - 2)):
+        send(p_send.at[1, 2 + i], p_recv.at[1, 2 + i], SKETCH + 1, at_y(d))
+
+    lax.fori_loop(tiles // 2, 3 * tiles // 4, turn, 0)
+
+    all_bytes(aux_recv, recv_sem.at[AUX]).wait()
+    near = [aux_recv[i] for i in range(4)]
+    near_cols = columns_of(near)
+    q_total, counts = q_cols[0], count
+    for i in range(4):
+        q_total = q_total + near_cols[i]
+        counts = counts + near[i][2:3, 0:1]
     to_scaled = lax.rsqrt((q_total + 1.0) / (counts + 1.0))
-    roots = {}
-    for d in y_order:
-        unit = jnp.exp2(aux_recv[d, 1:2, 0:1] * (1.0 / 256.0)) * (1.0 / 32767.0)
-        roots[d] = jnp.sqrt(jnp.maximum(q_cols[:, d:d + 1], 1e-30)) * unit
+    roots = [safe_root(near_cols[i]) * unit_of(near[i]) for i in range(4)]
+
+    def slot(d):
+        return order.index(d % NY)
 
     sketched = []
     for h in range(2):
-        all_bytes(p_recv.at[h, others], recv_sem.at[SKETCH + h]).wait()
-        raw = raw_own[:, h * HALF:(h + 1) * HALF]
-        for d in y_order:
-            raw = raw + p_recv[h, d].astype(jnp.int32).astype(F32) * roots[d]
+        all_bytes(p_recv.at[h], recv_sem.at[SKETCH + h]).wait()
+        raw = raws[0][:, h * HALF:(h + 1) * HALF]
+        for i in range(4):
+            raw = raw + p_recv[h, i].astype(jnp.int32).astype(F32) * roots[i]
         scaled = raw * to_scaled
         sketched.append(scaled)
-        w_all[h, NY - 1] = (scaled * to_scaled).astype(jnp.bfloat16)
-        for d in y_order:
-            send(w_all.at[h, NY - 1], w_all.at[h, order.index(NY - d)], ROWS + h, at_y(d))
+        w_all[h, slot(0)] = (scaled * to_scaled).astype(jnp.bfloat16)
+        for d, phase in ((2, ROWS_UP), (NY - 2, ROWS_DOWN), (1, ROWS_NEAR), (NY - 1, ROWS_NEAR)):
+            send(w_all.at[h, slot(0)], w_all.at[h, slot(-d)], phase + h, at_y(d))
+
+    def pass_on(h):
+        for phase, back, part in ((ROWS_UP, -2, pl.ds(0, CUT)), (ROWS_DOWN, 2, pl.ds(CUT, RY - CUT))):
+            ahead = -back // 2
+            held = w_all.at[h, slot(back)]
+            all_bytes(held, recv_sem.at[phase + h]).wait()
+            send(held.at[part], w_all.at[h, slot(2 * back), part], ROWS_FAR + h, at_y((2 * ahead) % NY))
+            send(held, w_all.at[h, slot(back - ahead)], ROWS_FAR + h, at_y(ahead % NY))
 
     sketched = jnp.concatenate(sketched, axis=1)
     own_gram = dot3(halves(sketched.T), halves(sketched), 0)
@@ -240,6 +310,8 @@
     for d in u_order:
         u1 = lax.rem(u + d, NU)
         send(g_own.at[pl.ds(pl.multiple_of(u1 * GX, 8), GX)], gx_recv.at[d], G_X, at_u(d))
+    lax.fori_loop(3 * tiles // 4, tiles, turn, 0)
+    pass_on(0)
     all_bytes(gx_recv.at[pl.ds(1, NU - 1)], recv_sem.at[G_X]).wait()
     total = g_own[pl.ds(pl.multiple_of(u * GX, 8), GX), :]
     for d in u_order:
@@ -289,7 +361,8 @@
         )
 
     def back_project(h):
-        all_bytes(w_all.at[h, pl.ds(0, NY - 1)], recv_sem.at[ROWS + h]).wait()
+        all_bytes(w_all.at[h, pl.ds(0, 2)], recv_sem.at[ROWS_NEAR + h]).wait()
+        all_bytes(w_all.at[h, pl.ds(0, 3)], recv_sem.at[ROWS_FAR + h]).wait()
         weights = w_all[h].reshape(rows, HALF)
         for d in x_order + [0]:
             x1 = lax.rem(x + d, NX)
@@ -353,6 +426,7 @@
             v = v + from_fixed(z_recv[h, d], TS)
         return v
 
+    pass_on(1)
     gram_along_y()
     back_project(0)
     first_along_x(0)
@@ -395,10 +469,15 @@
     out_ref[...] = dot3(halves(part), both, 1)
     gram_out.wait()
 
-    all_bytes(aux_send.at[others], send_sem.at[AUX]).wait()
+    all_bytes(fx_recv, send_sem.at[AUX_FAR]).wait()
+    all_bytes(f_send, send_sem.at[SKETCH_FAR]).wait()
+    all_bytes(aux_send, send_sem.at[AUX]).wait()
     for h in range(2):
-        all_bytes(p_send.at[h, others], send_sem.at[SKETCH + h]).wait()
-        all_bytes(w_all.at[h, pl.ds(0, NY - 1)], send_sem.at[ROWS + h]).wait()
+        all_bytes(p_send.at[h], send_sem.at[SKETCH + h]).wait()
+        all_bytes(w_all.at[h, pl.ds(0, 2)], send_sem.at[ROWS_NEAR + h]).wait()
+        all_bytes(w_all.at[h, 0], send_sem.at[ROWS_UP + h]).wait()
+        all_bytes(w_all.at[h, 0], send_sem.at[ROWS_DOWN + h]).wait()
+        all_bytes(w_all.at[h, pl.ds(0, 3)], send_sem.at[ROWS_FAR + h]).wait()
         all_bytes(x_send.at[h], send_sem.at[SUM_X + h]).wait()
         all_bytes(z_send.at[h, pl.ds(1, NZ - 1)], send_sem.at[SUM_Z + h]).wait()
     all_bytes(gx_recv.at[pl.ds(1, NU - 1)], send_sem.at[G_X]).wait()
@@ -474,10 +553,14 @@
                 pltpu.VMEM((cols, 128), jnp.bfloat16),
                 pltpu.VMEM((cols, rows), jnp.bfloat16),
                 pltpu.SemaphoreType.DMA((NY + 1,)),
-                pltpu.VMEM((2, NY, RY, HALF), i16),
-                pltpu.VMEM((2, NY, RY, HALF), i16),
-                pltpu.VMEM((NY, 8, 128), F32),
-                pltpu.VMEM((NY, 8, 128), F32),
+                pltpu.VMEM((3, RY, K), i16),
+                pltpu.VMEM((3, RY, K), i16),
+                pltpu.VMEM((3, 8, 128), F32),
+                pltpu.VMEM((4, 8, 128), F32),
+                pltpu.VMEM((2, 4, RY, HALF), i16),
+                pltpu.VMEM((2, 4, RY, HALF), i16),
+                pltpu.VMEM((4, 8, 128), F32),
+                pltpu.VMEM((4, 8, 128), F32),
                 pltpu.VMEM((2, NY, RY, HALF), jnp.bfloat16),
                 pltpu.VMEM((2 * K, 128), F32),
                 pltpu.VMEM((NU, GX, 128), F32),

time: 58.1 us -> 57.5 us (0.990)
  the two profiles are of different devices: /device:TPU:1 before, /device:TPU:8 now
where the time goes in v5:
time: 57.5 us; the launch traced here: 57.2 us
  Pallas kernels  57.2 us (99%)
    pallas_call x1, Pallas kernels, on_device(): pl.pallas_call(functools.partial(main_kernel, NX, NY, NZ, NC), out_shape=...  55.7 us
    pallas_call x1, Pallas kernels, on_device(): pl.pallas_call(last_kernel, out_shape=jax.ShapeDtypeStruct((TS, K), F32),...  1.53 us

profile of v5, /device:TPU:8, one launch (start us, length us, event | category | flops | bytes accessed | tf_op | source)
XLA Modules:
  0.0 57.2 jit_solution(3441358768718423356)
XLA Ops:
  0.0 55.7 %shard_map.37 = (f32[40,256]{1,0:T(8,128)}, f32[40,256]{1,0:T(8,128)}, f32[256,256]{1,0:T(8,128)}, f32[8,128]{1,0:T(8,128)}) custom-call(bf16[640,2560]{1,0:T(8,128)(2,1)} %depth_hbm.1, bf16[2560,256]{1,0:T(8,128)(2,1)} %gauss_hbm.1, s32[2560]{0:T(1024)} %keep_ref.1), custom_call_target="tpu_custom_call" | custom-call | tf_op jit(solution)/shard_map/pallas_call | solution.py:540
  55.7 1.5 %shard_map.38 = f32[40,256]{1,0:T(8,128)} custom-call(f32[40,256]{1,0:T(8,128)} %get-tuple-element.9.found_ref, f32[8,128]{1,0:T(8,128)} %get-tuple-element.10.off_ref, f32[40,256]{1,0:T(8,128)} %get-tuple-element.11.part_hbm, f32[256,256]{1,0:T(8,128)} %get-tuple-element.12.gram_hbm), custom_call_target="tpu_custom_call" | custom-call | tf_op jit(solution)/shard_map/pallas_call | solution.py:594

commit v6 on v5

--- a/solution.py
+++ b/solution.py
@@ -10,6 +10,7 @@
 MESH = pl.DeviceIdType.MESH
 F32 = jnp.float32
 HIGH = lax.Precision.HIGHEST
+STEPS = 3
 TOLERANCE = 2e-3
 HALF = 128
 AUX_FAR, SKETCH_FAR, AUX, SKETCH, G_X, G_Z, G_Y, G_BACK_Z, G_BACK_X, G_BACK_C = 0, 1, 2, 3, 5, 6, 7, 8, 9, 10
@@ -84,7 +85,7 @@
     NX, NY, NZ, NC,
     depth_hbm, gauss_hbm, keep_ref,
     out_ref, part_ref, gram_hbm, off_ref,
-    depth, gauss, keep_col, depth_t, load_sem,
+    depth, gauss, keep_col, depth_t, raw_sum, q_sum, inverse, load_sem,
     f_send, f_recv, fx_send, fx_recv, p_send, p_recv, aux_send, aux_recv, w_all,
     g_own, gx_recv, g_sum, gz_recv, g_piece, gy_recv, g_block, g_full, gram,
     terms, c_recv, own, h_send, h_recv, x_send, x_recv, z_send, z_recv,
@@ -132,7 +133,19 @@
             device_id=to, device_id_type=MESH,
         ).start()
 
-    y_order, u_order, z_order, x_order = far_first(NY), far_first(NU), far_first(NZ), far_first(NX)
+    y_order = far_first(NY)
+
+    def each_far_first(n, body):
+        def step(i, _):
+            k = (i + 1) // 2
+            body(n // 2 + jnp.where(lax.rem(i, 2) == 0, k, -k))
+            return 0
+
+        lax.fori_loop(0, n - 1, step, 0)
+
+    def sum_over(n, first, ref):
+        return lax.fori_loop(1, n, lambda d, total: total + ref[d], first)
+
     others = pl.ds(1, NY - 1)
 
     def row_block(y1):
@@ -150,12 +163,9 @@
         loads.append(load)
 
     barrier = pltpu.get_barrier_semaphore()
-    for d in y_order:
-        pl.semaphore_signal(barrier, inc=1, device_id=at_y(d), device_id_type=MESH)
-    for d in u_order:
-        pl.semaphore_signal(barrier, inc=1, device_id=at_u(d), device_id_type=MESH)
-    for d in z_order:
-        pl.semaphore_signal(barrier, inc=1, device_id=at_z(d), device_id_type=MESH)
+    for n, at in ((NY, at_y), (NU, at_u), (NZ, at_z)):
+        each_far_first(n, lambda d, at=at: pl.semaphore_signal(
+            barrier, inc=1, device_id=at(d), device_id_type=MESH))
 
     kept = keep_ref[...].astype(F32).reshape(1, cols)
     count = jnp.sum(kept, axis=1, keepdims=True)
@@ -164,11 +174,15 @@
         tile = jnp.broadcast_to(kept[:, j * 128:(j + 1) * 128], (128, 128)).T
         keep_col[j * 128:(j + 1) * 128, :] = tile.astype(jnp.bfloat16)
     gauss_load.wait()
-    for j in range(cols // 128):
-        at = slice(j * 128, (j + 1) * 128)
+    tiles = cols // 128
+
+    def filter_rows(j, _):
+        at = pl.ds(pl.multiple_of(j * 128, 128), 128)
         tile = keep_col[at, :]
-        for h in range(2):
-            gauss[at, h * HALF:(h + 1) * HALF] = gauss[at, h * HALF:(h + 1) * HALF] * tile
+        gauss[at, :] = gauss[at, :] * jnp.concatenate([tile] * (K // 128), axis=1)
+        return 0
+
+    lax.fori_loop(0, tiles, filter_rows, 0)
 
     def aux_of(q_row, code, number):
         return jnp.where(sub == 0, q_row, jnp.where(sub == 1, code, jnp.where(sub == 2, number, 0.0)))
@@ -201,9 +215,20 @@
     for g in range(2):
         for i in range(g * group, (g + 1) * group):
             loads[i].wait()
-        values = depth[g * group * RY:(g + 1) * group * RY, :]
-        raw = jnp.dot(values, gauss[...], preferred_element_type=F32)
-        q = jnp.dot(values * values, keep_col[...], preferred_element_type=F32)
+        span = slice(g * group * RY, (g + 1) * group * RY)
+        raw_sum[...] = jnp.zeros_like(raw_sum)
+        q_sum[...] = jnp.zeros_like(q_sum)
+
+        def add_columns(j, _):
+            at = pl.ds(pl.multiple_of(j * 256, 256), 256)
+            values = depth[span, at]
+            raw_sum[...] += jnp.dot(values, gauss[at, :], preferred_element_type=F32)
+            q_sum[...] += jnp.dot(values * values, keep_col[at, :], preferred_element_type=F32)
+            return 0
+
+        lax.fori_loop(0, cols // 256, add_columns, 0)
+        raw = raw_sum[...]
+        q = q_sum[...]
         for i in range(group):
             d = order[g * group + i]
             at = slice(i * RY, (i + 1) * RY)
@@ -236,7 +261,6 @@
                 for h in range(2):
                     send(p_send.at[h, i], p_recv.at[h, i], SKETCH + h, at_y(d))
 
-    tiles = cols // 128
     lax.fori_loop(0, tiles // 2, turn, 0)
 
     all_bytes(fx_recv, recv_sem.at[AUX_FAR]).wait()
@@ -307,45 +331,38 @@
     own_gram = dot3(halves(sketched.T), halves(sketched), 0)
     g_own[0:K, :] = own_gram[:, :HALF]
     g_own[K:2 * K, :] = own_gram[:, HALF:]
-    for d in u_order:
+    def send_x(d):
         u1 = lax.rem(u + d, NU)
         send(g_own.at[pl.ds(pl.multiple_of(u1 * GX, 8), GX)], gx_recv.at[d], G_X, at_u(d))
+
+    each_far_first(NU, send_x)
     lax.fori_loop(3 * tiles // 4, tiles, turn, 0)
     pass_on(0)
     all_bytes(gx_recv.at[pl.ds(1, NU - 1)], recv_sem.at[G_X]).wait()
-    total = g_own[pl.ds(pl.multiple_of(u * GX, 8), GX), :]
-    for d in u_order:
-        total = total + gx_recv[d]
-    g_sum[...] = total
-    for d in z_order:
+    g_sum[...] = sum_over(NU, g_own[pl.ds(pl.multiple_of(u * GX, 8), GX), :], gx_recv)
+
+    def send_z(d):
         z1 = lax.rem(z + d, NZ)
         send(g_sum.at[pl.ds(pl.multiple_of(z1 * GZ, 8), GZ)], gz_recv.at[d], G_Z, at_z(d))
 
+    each_far_first(NZ, send_z)
+
     def gram_along_y():
         all_bytes(gz_recv.at[pl.ds(1, NZ - 1)], recv_sem.at[G_Z]).wait()
-        piece = g_sum[pl.ds(pl.multiple_of(z * GZ, 8), GZ), :]
-        for d in z_order:
-            piece = piece + gz_recv[d]
-        g_piece[...] = piece
-        for d in y_order:
-            send(g_piece, gy_recv.at[d], G_Y, at_y(d))
+        g_piece[...] = sum_over(NZ, g_sum[pl.ds(pl.multiple_of(z * GZ, 8), GZ), :], gz_recv)
+        each_far_first(NY, lambda d: send(g_piece, gy_recv.at[d], G_Y, at_y(d)))
 
     def gram_back_along_z():
         all_bytes(gy_recv.at[others], recv_sem.at[G_Y]).wait()
-        piece = g_piece[...]
-        for d in y_order:
-            piece = piece + gy_recv[d]
         here = pl.ds(pl.multiple_of(z * GZ, 8), GZ)
-        g_block[here, :] = piece
-        for d in z_order:
-            send(g_block.at[here], g_block.at[here], G_BACK_Z, at_z(d))
+        g_block[here, :] = sum_over(NY, g_piece[...], gy_recv)
+        each_far_first(NZ, lambda d: send(g_block.at[here], g_block.at[here], G_BACK_Z, at_z(d)))
 
     def gram_back_along_x():
         all_bytes(g_block.at[pl.ds(0, GX - GZ)], recv_sem.at[G_BACK_Z]).wait()
         there = pl.ds(pl.multiple_of(u * GX, 8), GX)
         g_full[there, :] = g_block[...]
-        for d in x_order:
-            send(g_block, g_full.at[there], G_BACK_X, at_x(d))
+        each_far_first(NX, lambda d: send(g_block, g_full.at[there], G_BACK_X, at_x(d)))
 
     side = pl.ds(pl.multiple_of(core * (NX * GX), 8), NX * GX)
 
@@ -364,12 +381,17 @@
         all_bytes(w_all.at[h, pl.ds(0, 2)], recv_sem.at[ROWS_NEAR + h]).wait()
         all_bytes(w_all.at[h, pl.ds(0, 3)], recv_sem.at[ROWS_FAR + h]).wait()
         weights = w_all[h].reshape(rows, HALF)
-        for d in x_order + [0]:
+
+        def one(i, _):
+            d = lax.rem(NX // 2 + i, NX)
             x1 = lax.rem(x + d, NX)
             block = depth_t[pl.ds(pl.multiple_of(x1 * (XB * NC), 16), XB * NC), :]
             product = jnp.dot(block, weights, preferred_element_type=F32)
             terms[h, d] = product.reshape(NZ, NC, TS, HALF)
             core_copy(h, d).start()
+            return 0
+
+        lax.fori_loop(0, NX, one, 0)
 
     ways = ((0, 1), (1, NX - 1))
 
@@ -381,18 +403,24 @@
         )
 
     def first_along_x(h):
-        for i, d in enumerate(x_order + [0]):
+        def both_cores(d):
             core_copy(h, d).wait()
-            half = (terms[h, d, :, core] + c_recv[h, d]).reshape(XB, HALF)
-            if i > 0:
-                own[h, d] = half
-                continue
-            code = scale_code(whole_max(half))
-            fixed = to_fixed(half, code)
-            for slot, to in ways:
-                h_send[h, slot, 0:H, :] = fixed[slot * H:(slot + 1) * H]
-                h_send[h, slot, H:H + 16, :] = code_rows(code, HALF)
-                way_copy(h, slot, to).start()
+            return (terms[h, d, :, core] + c_recv[h, d]).reshape(XB, HALF)
+
+        half = both_cores(NX // 2)
+        code = scale_code(whole_max(half))
+        fixed = to_fixed(half, code)
+        for slot, to in ways:
+            h_send[h, slot, 0:H, :] = fixed[slot * H:(slot + 1) * H]
+            h_send[h, slot, H:H + 16, :] = code_rows(code, HALF)
+            way_copy(h, slot, to).start()
+
+        def rest(i, _):
+            d = lax.rem(NX // 2 + i, NX)
+            own[h, d] = both_cores(d)
+            return 0
+
+        lax.fori_loop(1, NX, rest, 0)
 
     def second_along_x(h):
         for slot, to in ways:
@@ -412,19 +440,20 @@
         unit = 32767.0 * jnp.exp2(code * (-1.0 / 256.0))
         tail = jnp.broadcast_to(code, (8, HALF))
         own[h, 0] = half
-        for d in z_order:
+
+        def one(d):
             z1 = lax.rem(z + d, NZ)
             v = own[h, 0, pl.ds(pl.multiple_of(z1 * TS, 8), TS), :]
             v = jnp.concatenate([v * unit, tail], axis=0)
             z_send[h, d] = v.astype(jnp.int32).astype(jnp.int16)
             send(z_send.at[h, d], z_recv.at[h, d], SUM_Z + h, at_z(d))
 
+        each_far_first(NZ, one)
+
     def total_along_z(h):
         all_bytes(z_recv.at[h, pl.ds(1, NZ - 1)], recv_sem.at[SUM_Z + h]).wait()
         v = own[h, 0, pl.ds(pl.multiple_of(z * TS, 8), TS), :]
-        for d in z_order:
-            v = v + from_fixed(z_recv[h, d], TS)
-        return v
+        return lax.fori_loop(1, NZ, lambda d, v: v + from_fixed(z_recv[h, d], TS), v)
 
     pass_on(1)
     gram_along_y()
@@ -452,17 +481,17 @@
     d_col = lax.rsqrt(jnp.sum(diagonal, axis=1, keepdims=True))
     unit_gram = matrix * d_row * d_col
     unit_halves = halves(unit_gram)
-    inverse = eye - half_lower(unit_gram - eye)
-    rough = inverse.astype(jnp.bfloat16)
-    error = dot(dot(rough, unit_halves[0], 0).astype(jnp.bfloat16), rough, 1) - eye
-    inverse = inverse - dot(half_lower(error).astype(jnp.bfloat16), rough, 0)
-    for _ in range(2):
-        both = halves(inverse)
+    inverse[...] = eye - half_lower(unit_gram - eye)
+
+    def improve(i, _):
+        both = halves(inverse[...])
         error = dot3(halves(dot3(both, unit_halves, 0)), both, 1) - eye
-        inverse = inverse - dot(half_lower(error).astype(jnp.bfloat16), both[0], 0)
-    inverse = inverse * d_row
-    off_ref[...] = jnp.broadcast_to(whole_max(error), (8, 128))
-    both = halves(inverse)
+        off_ref[...] = jnp.broadcast_to(whole_max(error), (8, 128))
+        inverse[...] = inverse[...] - dot(half_lower(error).astype(jnp.bfloat16), both[0], 0)
+        return 0
+
+    lax.fori_loop(0, STEPS, improve, 0)
+    both = halves(inverse[...] * d_row)
 
     part = jnp.concatenate([total_along_z(0), total_along_z(1)], axis=1)
     part_ref[...] = part
@@ -552,6 +581,9 @@
                 pltpu.VMEM((cols, K), jnp.bfloat16),
                 pltpu.VMEM((cols, 128), jnp.bfloat16),
                 pltpu.VMEM((cols, rows), jnp.bfloat16),
+                pltpu.VMEM((rows // 2, K), F32),
+                pltpu.VMEM((rows // 2, 128), F32),
+                pltpu.VMEM((K, K), F32),
                 pltpu.SemaphoreType.DMA((NY + 1,)),
                 pltpu.VMEM((3, RY, K), i16),
                 pltpu.VMEM((3, RY, K), i16),

time: 57.5 us -> 57.9 us (level)
  no operation moved by 1% of the time
where the time goes in v6:
time: 57.9 us; the launch traced here: 57.6 us
  Pallas kernels  57.6 us (99%)
    pallas_call x1, Pallas kernels, on_device(): pl.pallas_call(functools.partial(main_kernel, NX, NY, NZ, NC), out_shape=...  56.1 us
    pallas_call x1, Pallas kernels, on_device(): pl.pallas_call(last_kernel, out_shape=jax.ShapeDtypeStruct((TS, K), F32),...  1.53 us

profile of v6, /device:TPU:8, one launch (start us, length us, event | category | flops | bytes accessed | tf_op | source)
XLA Modules:
  0.0 57.6 jit_solution(14898927180275443566)
XLA Ops:
  0.0 56.1 %shard_map.37 = (f32[40,256]{1,0:T(8,128)}, f32[40,256]{1,0:T(8,128)}, f32[256,256]{1,0:T(8,128)}, f32[8,128]{1,0:T(8,128)}) custom-call(bf16[640,2560]{1,0:T(8,128)(2,1)} %depth_hbm.1, bf16[2560,256]{1,0:T(8,128)(2,1)} %gauss_hbm.1, s32[2560]{0:T(1024)} %keep_ref.1), custom_call_target="tpu_custom_call" | custom-call | tf_op jit(solution)/shard_map/pallas_call | solution.py:569
  56.1 1.5 %shard_map.38 = f32[40,256]{1,0:T(8,128)} custom-call(f32[40,256]{1,0:T(8,128)} %get-tuple-element.9.found_ref, f32[8,128]{1,0:T(8,128)} %get-tuple-element.10.off_ref, f32[40,256]{1,0:T(8,128)} %get-tuple-element.11.part_hbm, f32[256,256]{1,0:T(8,128)} %get-tuple-element.12.gram_hbm), custom_call_target="tpu_custom_call" | custom-call | tf_op jit(solution)/shard_map/pallas_call | solution.py:626

commit v7 on v6

--- a/solution.py
+++ b/solution.py
@@ -10,8 +10,7 @@
 MESH = pl.DeviceIdType.MESH
 F32 = jnp.float32
 HIGH = lax.Precision.HIGHEST
-STEPS = 3
-TOLERANCE = 2e-3
+TOLERANCE = 1e-2
 HALF = 128
 AUX_FAR, SKETCH_FAR, AUX, SKETCH, G_X, G_Z, G_Y, G_BACK_Z, G_BACK_X, G_BACK_C = 0, 1, 2, 3, 5, 6, 7, 8, 9, 10
 SUM_X, SUM_Z, ROWS_NEAR, ROWS_UP, ROWS_DOWN, ROWS_FAR, PHASES = 11, 13, 15, 17, 19, 21, 23
@@ -261,7 +260,7 @@
                 for h in range(2):
                     send(p_send.at[h, i], p_recv.at[h, i], SKETCH + h, at_y(d))
 
-    lax.fori_loop(0, tiles // 2, turn, 0)
+    lax.fori_loop(0, tiles // 4, turn, 0)
 
     all_bytes(fx_recv, recv_sem.at[AUX_FAR]).wait()
     all_bytes(f_recv, recv_sem.at[SKETCH_FAR]).wait()
@@ -292,7 +291,7 @@
     for i, d in ((0, 2), (1, NY - 2)):
         send(p_send.at[1, 2 + i], p_recv.at[1, 2 + i], SKETCH + 1, at_y(d))
 
-    lax.fori_loop(tiles // 2, 3 * tiles // 4, turn, 0)
+    lax.fori_loop(tiles // 4, tiles // 2, turn, 0)
 
     all_bytes(aux_recv, recv_sem.at[AUX]).wait()
     near = [aux_recv[i] for i in range(4)]
@@ -336,8 +335,10 @@
         send(g_own.at[pl.ds(pl.multiple_of(u1 * GX, 8), GX)], gx_recv.at[d], G_X, at_u(d))
 
     each_far_first(NU, send_x)
+    lax.fori_loop(tiles // 2, 3 * tiles // 4, turn, 0)
+    pass_on(0)
+    pass_on(1)
     lax.fori_loop(3 * tiles // 4, tiles, turn, 0)
-    pass_on(0)
     all_bytes(gx_recv.at[pl.ds(1, NU - 1)], recv_sem.at[G_X]).wait()
     g_sum[...] = sum_over(NU, g_own[pl.ds(pl.multiple_of(u * GX, 8), GX), :], gx_recv)
 
@@ -455,19 +456,18 @@
         v = own[h, 0, pl.ds(pl.multiple_of(z * TS, 8), TS), :]
         return lax.fori_loop(1, NZ, lambda d, v: v + from_fixed(z_recv[h, d], TS), v)
 
-    pass_on(1)
+    back_project(0)
+    back_project(1)
     gram_along_y()
-    back_project(0)
     first_along_x(0)
-    back_project(1)
+    first_along_x(1)
     second_along_x(0)
     gram_back_along_z()
-    first_along_x(1)
+    second_along_x(1)
+    along_z(0)
     gram_back_along_x()
-    along_z(0)
-    second_along_x(1)
+    along_z(1)
     gram_back_to_core()
-    along_z(1)
 
     all_bytes(g_full.at[pl.ds(0, NX * GX)], recv_sem.at[G_BACK_C]).wait()
     gram[:, 0:128] = g_full[0:K, :]
@@ -481,17 +481,15 @@
     d_col = lax.rsqrt(jnp.sum(diagonal, axis=1, keepdims=True))
     unit_gram = matrix * d_row * d_col
     unit_halves = halves(unit_gram)
-    inverse[...] = eye - half_lower(unit_gram - eye)
-
-    def improve(i, _):
-        both = halves(inverse[...])
-        error = dot3(halves(dot3(both, unit_halves, 0)), both, 1) - eye
-        off_ref[...] = jnp.broadcast_to(whole_max(error), (8, 128))
-        inverse[...] = inverse[...] - dot(half_lower(error).astype(jnp.bfloat16), both[0], 0)
-        return 0
-
-    lax.fori_loop(0, STEPS, improve, 0)
-    both = halves(inverse[...] * d_row)
+    start = eye - half_lower(unit_gram - eye)
+    rough = start.astype(jnp.bfloat16)
+    error = dot(dot(rough, unit_halves[0], 0).astype(jnp.bfloat16), rough, 1) - eye
+    inverse[...] = start - dot(half_lower(error).astype(jnp.bfloat16), rough, 0)
+    both = halves(inverse[...])
+    error = dot3(halves(dot3(both, unit_halves, 0)), both, 1) - eye
+    off_ref[...] = jnp.broadcast_to(whole_max(error), (8, 128))
+    found = inverse[...] - dot(half_lower(error).astype(jnp.bfloat16), both[0], 0)
+    both = halves(found * d_row)
 
     part = jnp.concatenate([total_along_z(0), total_along_z(1)], axis=1)
     part_ref[...] = part

time: 57.9 us -> 55.5 us (0.959)
  the two profiles are of different devices: /device:TPU:8 before, /device:TPU:1 now
where the time goes in v7:
time: 55.5 us; the launch traced here: 55.2 us
  Pallas kernels  55.2 us (99%)
    pallas_call x1, Pallas kernels, on_device(): pl.pallas_call(functools.partial(main_kernel, NX, NY, NZ, NC), out_shape=...  53.7 us
    pallas_call x1, Pallas kernels, on_device(): pl.pallas_call(last_kernel, out_shape=jax.ShapeDtypeStruct((TS, K), F32),...  1.53 us

profile of v7, /device:TPU:1, one launch (start us, length us, event | category | flops | bytes accessed | tf_op | source)
XLA Modules:
  0.0 55.2 jit_solution(3587101329842659896)
XLA Ops:
  0.0 53.7 %shard_map.37 = (f32[40,256]{1,0:T(8,128)}, f32[40,256]{1,0:T(8,128)}, f32[256,256]{1,0:T(8,128)}, f32[8,128]{1,0:T(8,128)}) custom-call(bf16[640,2560]{1,0:T(8,128)(2,1)} %depth_hbm.1, bf16[2560,256]{1,0:T(8,128)(2,1)} %gauss_hbm.1, s32[2560]{0:T(1024)} %keep_ref.1), custom_call_target="tpu_custom_call" | custom-call | tf_op jit(solution)/shard_map/pallas_call | solution.py:567
  53.7 1.5 %shard_map.38 = f32[40,256]{1,0:T(8,128)} custom-call(f32[40,256]{1,0:T(8,128)} %get-tuple-element.9.found_ref, f32[8,128]{1,0:T(8,128)} %get-tuple-element.10.off_ref, f32[40,256]{1,0:T(8,128)} %get-tuple-element.11.part_hbm, f32[256,256]{1,0:T(8,128)} %get-tuple-element.12.gram_hbm), custom_call_target="tpu_custom_call" | custom-call | tf_op jit(solution)/shard_map/pallas_call | solution.py:624

commit v8 on v7

--- a/solution.py
+++ b/solution.py
@@ -175,14 +175,6 @@
     gauss_load.wait()
     tiles = cols // 128
 
-    def filter_rows(j, _):
-        at = pl.ds(pl.multiple_of(j * 128, 128), 128)
-        tile = keep_col[at, :]
-        gauss[at, :] = gauss[at, :] * jnp.concatenate([tile] * (K // 128), axis=1)
-        return 0
-
-    lax.fori_loop(0, tiles, filter_rows, 0)
-
     def aux_of(q_row, code, number):
         return jnp.where(sub == 0, q_row, jnp.where(sub == 1, code, jnp.where(sub == 2, number, 0.0)))
 
@@ -220,6 +212,8 @@
 
         def add_columns(j, _):
             at = pl.ds(pl.multiple_of(j * 256, 256), 256)
+            if g == 0:
+                gauss[at, :] = gauss[at, :] * jnp.concatenate([keep_col[at, :]] * (K // 128), axis=1)
             values = depth[span, at]
             raw_sum[...] += jnp.dot(values, gauss[at, :], preferred_element_type=F32)
             q_sum[...] += jnp.dot(values * values, keep_col[at, :], preferred_element_type=F32)
@@ -254,11 +248,10 @@
         else:
             for i, d in enumerate((1, NY - 1)):
                 for h in range(2):
-                    p_send[h, i] = fixed[h][i * RY:(i + 1) * RY]
+                    p_send[i, :, h * HALF:(h + 1) * HALF] = fixed[h][i * RY:(i + 1) * RY]
                 aux_send[i] = aux_of(q_rows[d], code, count)
                 send(aux_send.at[i], aux_recv.at[i], AUX, at_y(d))
-                for h in range(2):
-                    send(p_send.at[h, i], p_recv.at[h, i], SKETCH + h, at_y(d))
+                send(p_send.at[i], p_recv.at[i], SKETCH, at_y(d))
 
     lax.fori_loop(0, tiles // 4, turn, 0)
 
@@ -285,11 +278,8 @@
         fixed = to_fixed(level, code)
         aux_send[2 + i] = aux_of(q_row, code, number)
         send(aux_send.at[2 + i], aux_recv.at[2 + i], AUX, at_y(d))
-        for h in range(2):
-            p_send[h, 2 + i] = fixed[:, h * HALF:(h + 1) * HALF]
-        send(p_send.at[0, 2 + i], p_recv.at[0, 2 + i], SKETCH, at_y(d))
-    for i, d in ((0, 2), (1, NY - 2)):
-        send(p_send.at[1, 2 + i], p_recv.at[1, 2 + i], SKETCH + 1, at_y(d))
+        p_send[2 + i] = fixed
+        send(p_send.at[2 + i], p_recv.at[2 + i], SKETCH, at_y(d))
 
     lax.fori_loop(tiles // 4, tiles // 2, turn, 0)
 
@@ -306,27 +296,23 @@
     def slot(d):
         return order.index(d % NY)
 
-    sketched = []
-    for h in range(2):
-        all_bytes(p_recv.at[h], recv_sem.at[SKETCH + h]).wait()
-        raw = raws[0][:, h * HALF:(h + 1) * HALF]
-        for i in range(4):
-            raw = raw + p_recv[h, i].astype(jnp.int32).astype(F32) * roots[i]
-        scaled = raw * to_scaled
-        sketched.append(scaled)
-        w_all[h, slot(0)] = (scaled * to_scaled).astype(jnp.bfloat16)
-        for d, phase in ((2, ROWS_UP), (NY - 2, ROWS_DOWN), (1, ROWS_NEAR), (NY - 1, ROWS_NEAR)):
-            send(w_all.at[h, slot(0)], w_all.at[h, slot(-d)], phase + h, at_y(d))
-
-    def pass_on(h):
+    all_bytes(p_recv, recv_sem.at[SKETCH]).wait()
+    raw = raws[0]
+    for i in range(4):
+        raw = raw + p_recv[i].astype(jnp.int32).astype(F32) * roots[i]
+    sketched = raw * to_scaled
+    w_all[slot(0)] = (sketched * to_scaled).astype(jnp.bfloat16)
+    for d, phase in ((2, ROWS_UP), (NY - 2, ROWS_DOWN), (1, ROWS_NEAR), (NY - 1, ROWS_NEAR)):
+        send(w_all.at[slot(0)], w_all.at[slot(-d)], phase, at_y(d))
+
+    def pass_on():
         for phase, back, part in ((ROWS_UP, -2, pl.ds(0, CUT)), (ROWS_DOWN, 2, pl.ds(CUT, RY - CUT))):
             ahead = -back // 2
-            held = w_all.at[h, slot(back)]
-            all_bytes(held, recv_sem.at[phase + h]).wait()
-            send(held.at[part], w_all.at[h, slot(2 * back), part], ROWS_FAR + h, at_y((2 * ahead) % NY))
-            send(held, w_all.at[h, slot(back - ahead)], ROWS_FAR + h, at_y(ahead % NY))
-
-    sketched = jnp.concatenate(sketched, axis=1)
+            held = w_all.at[slot(back)]
+            all_bytes(held, recv_sem.at[phase]).wait()
+            send(held.at[part], w_all.at[slot(2 * back), part], ROWS_FAR, at_y((2 * ahead) % NY))
+            send(held, w_all.at[slot(back - ahead)], ROWS_FAR, at_y(ahead % NY))
+
     own_gram = dot3(halves(sketched.T), halves(sketched), 0)
     g_own[0:K, :] = own_gram[:, :HALF]
     g_own[K:2 * K, :] = own_gram[:, HALF:]
@@ -336,8 +322,7 @@
 
     each_far_first(NU, send_x)
     lax.fori_loop(tiles // 2, 3 * tiles // 4, turn, 0)
-    pass_on(0)
-    pass_on(1)
+    pass_on()
     lax.fori_loop(3 * tiles // 4, tiles, turn, 0)
     all_bytes(gx_recv.at[pl.ds(1, NU - 1)], recv_sem.at[G_X]).wait()
     g_sum[...] = sum_over(NU, g_own[pl.ds(pl.multiple_of(u * GX, 8), GX), :], gx_recv)
@@ -378,18 +363,18 @@
             device_id=at_core(), device_id_type=MESH,
         )
 
-    def back_project(h):
-        all_bytes(w_all.at[h, pl.ds(0, 2)], recv_sem.at[ROWS_NEAR + h]).wait()
-        all_bytes(w_all.at[h, pl.ds(0, 3)], recv_sem.at[ROWS_FAR + h]).wait()
-        weights = w_all[h].reshape(rows, HALF)
+    def back_project():
+        all_bytes(w_all.at[pl.ds(0, 2)], recv_sem.at[ROWS_NEAR]).wait()
+        all_bytes(w_all.at[pl.ds(0, 3)], recv_sem.at[ROWS_FAR]).wait()
 
         def one(i, _):
             d = lax.rem(NX // 2 + i, NX)
             x1 = lax.rem(x + d, NX)
             block = depth_t[pl.ds(pl.multiple_of(x1 * (XB * NC), 16), XB * NC), :]
-            product = jnp.dot(block, weights, preferred_element_type=F32)
-            terms[h, d] = product.reshape(NZ, NC, TS, HALF)
-            core_copy(h, d).start()
+            product = jnp.dot(block, w_all[...].reshape(rows, K), preferred_element_type=F32)
+            for h in range(2):
+                terms[h, d] = product[:, h * HALF:(h + 1) * HALF].reshape(NZ, NC, TS, HALF)
+                core_copy(h, d).start()
             return 0
 
         lax.fori_loop(0, NX, one, 0)
@@ -456,8 +441,7 @@
         v = own[h, 0, pl.ds(pl.multiple_of(z * TS, 8), TS), :]
         return lax.fori_loop(1, NZ, lambda d, v: v + from_fixed(z_recv[h, d], TS), v)
 
-    back_project(0)
-    back_project(1)
+    back_project()
     gram_along_y()
     first_along_x(0)
     first_along_x(1)
@@ -499,12 +483,12 @@
     all_bytes(fx_recv, send_sem.at[AUX_FAR]).wait()
     all_bytes(f_send, send_sem.at[SKETCH_FAR]).wait()
     all_bytes(aux_send, send_sem.at[AUX]).wait()
+    all_bytes(p_send, send_sem.at[SKETCH]).wait()
+    all_bytes(w_all.at[pl.ds(0, 2)], send_sem.at[ROWS_NEAR]).wait()
+    all_bytes(w_all.at[0], send_sem.at[ROWS_UP]).wait()
+    all_bytes(w_all.at[0], send_sem.at[ROWS_DOWN]).wait()
+    all_bytes(w_all.at[pl.ds(0, 3)], send_sem.at[ROWS_FAR]).wait()
     for h in range(2):
-        all_bytes(p_send.at[h], send_sem.at[SKETCH + h]).wait()
-        all_bytes(w_all.at[h, pl.ds(0, 2)], send_sem.at[ROWS_NEAR + h]).wait()
-        all_bytes(w_all.at[h, 0], send_sem.at[ROWS_UP + h]).wait()
-        all_bytes(w_all.at[h, 0], send_sem.at[ROWS_DOWN + h]).wait()
-        all_bytes(w_all.at[h, pl.ds(0, 3)], send_sem.at[ROWS_FAR + h]).wait()
         all_bytes(x_send.at[h], send_sem.at[SUM_X + h]).wait()
         all_bytes(z_send.at[h, pl.ds(1, NZ - 1)], send_sem.at[SUM_Z + h]).wait()
     all_bytes(gx_recv.at[pl.ds(1, NU - 1)], send_sem.at[G_X]).wait()
@@ -587,11 +571,11 @@
                 pltpu.VMEM((3, RY, K), i16),
                 pltpu.VMEM((3, 8, 128), F32),
                 pltpu.VMEM((4, 8, 128), F32),
-                pltpu.VMEM((2, 4, RY, HALF), i16),
-                pltpu.VMEM((2, 4, RY, HALF), i16),
+                pltpu.VMEM((4, RY, K), i16),
+                pltpu.VMEM((4, RY, K), i16),
                 pltpu.VMEM((4, 8, 128), F32),
                 pltpu.VMEM((4, 8, 128), F32),
-                pltpu.VMEM((2, NY, RY, HALF), jnp.bfloat16),
+                pltpu.VMEM((NY, RY, K), jnp.bfloat16),
                 pltpu.VMEM((2 * K, 128), F32),
                 pltpu.VMEM((NU, GX, 128), F32),
                 pltpu.VMEM((GX, 128), F32),

time: 55.5 us -> 55.1 us (level)
  no operation moved by 1% of the time
where the time goes in v8:
time: 55.1 us; the launch traced here: 54.9 us
  Pallas kernels  54.9 us (100%)
    pallas_call x1, Pallas kernels, on_device(): pl.pallas_call(functools.partial(main_kernel, NX, NY, NZ, NC), out_shape=...  53.4 us
    pallas_call x1, Pallas kernels, on_device(): pl.pallas_call(last_kernel, out_shape=jax.ShapeDtypeStruct((TS, K), F32),...  1.53 us

profile of v8, /device:TPU:1, one launch (start us, length us, event | category | flops | bytes accessed | tf_op | source)
XLA Modules:
  0.0 54.9 jit_solution(14609957474531112642)
XLA Ops:
  0.0 53.4 %shard_map.37 = (f32[40,256]{1,0:T(8,128)}, f32[40,256]{1,0:T(8,128)}, f32[256,256]{1,0:T(8,128)}, f32[8,128]{1,0:T(8,128)}) custom-call(bf16[640,2560]{1,0:T(8,128)(2,1)} %depth_hbm.1, bf16[2560,256]{1,0:T(8,128)(2,1)} %gauss_hbm.1, s32[2560]{0:T(1024)} %keep_ref.1), custom_call_target="tpu_custom_call" | custom-call | tf_op jit(solution)/shard_map/pallas_call | solution.py:551
  53.4 1.5 %shard_map.38 = f32[40,256]{1,0:T(8,128)} custom-call(f32[40,256]{1,0:T(8,128)} %get-tuple-element.9.found_ref, f32[8,128]{1,0:T(8,128)} %get-tuple-element.10.off_ref, f32[40,256]{1,0:T(8,128)} %get-tuple-element.11.part_hbm, f32[256,256]{1,0:T(8,128)} %get-tuple-element.12.gram_hbm), custom_call_target="tpu_custom_call" | custom-call | tf_op jit(solution)/shard_map/pallas_call | solution.py:608

commit v9 on v8

--- a/solution.py
+++ b/solution.py
@@ -453,6 +453,8 @@
     along_z(1)
     gram_back_to_core()
 
+    left_part = total_along_z(0)
+
     all_bytes(g_full.at[pl.ds(0, NX * GX)], recv_sem.at[G_BACK_C]).wait()
     gram[:, 0:128] = g_full[0:K, :]
     gram[:, 128:256] = g_full[K:2 * K, :]
@@ -475,7 +477,7 @@
     found = inverse[...] - dot(half_lower(error).astype(jnp.bfloat16), both[0], 0)
     both = halves(found * d_row)
 
-    part = jnp.concatenate([total_along_z(0), total_along_z(1)], axis=1)
+    part = jnp.concatenate([left_part, total_along_z(1)], axis=1)
     part_ref[...] = part
     out_ref[...] = dot3(halves(part), both, 1)
     gram_out.wait()
@@ -499,10 +501,15 @@
     all_bytes(g_full.at[side], send_sem.at[G_BACK_C]).wait()
 
 
-def last_kernel(found_ref, off_ref, part_hbm, gram_hbm, out_ref, work, right, part, sem):
+def last_kernel(found_hbm, off_hbm, part_hbm, gram_hbm, out_hbm, off, work, right, part, out, sem, take_sem):
     K = work.shape[0]
-    settled = jnp.max(off_ref[...]) < TOLERANCE
-    out_ref[...] = found_ref[...]
+    take = pltpu.make_async_copy(found_hbm, out_hbm, take_sem)
+    take.start()
+    load = pltpu.make_async_copy(off_hbm, off, sem)
+    load.start()
+    load.wait()
+    settled = jnp.max(off[...]) < TOLERANCE
+    take.wait()
 
     @pl.when(jnp.logical_not(settled))
     def _():
@@ -530,7 +537,10 @@
 
         lax.fori_loop(0, K, step, 0)
         pivots = jnp.sum(work[...] * identity(K), axis=1, keepdims=True)
-        out_ref[...] = times_t(part[...], right[...] / jnp.sqrt(pivots))
+        out[...] = times_t(part[...], right[...] / jnp.sqrt(pivots))
+        store = pltpu.make_async_copy(out, out_hbm, sem)
+        store.start()
+        store.wait()
 
 
 def solution(mesh, sizes=(4, 8, 8, 2)):
@@ -608,12 +618,15 @@
         return pl.pallas_call(
             last_kernel,
             out_shape=jax.ShapeDtypeStruct((TS, K), F32),
-            in_specs=[vmem, vmem, hbm, hbm],
-            out_specs=vmem,
+            in_specs=[hbm, hbm, hbm, hbm],
+            out_specs=hbm,
             scratch_shapes=[
+                pltpu.VMEM((8, 128), F32),
                 pltpu.VMEM((K, K), F32),
                 pltpu.VMEM((K, K), F32),
                 pltpu.VMEM((TS, K), F32),
+                pltpu.VMEM((TS, K), F32),
+                pltpu.SemaphoreType.DMA,
                 pltpu.SemaphoreType.DMA,
             ],
             compiler_params=pltpu.CompilerParams(vmem_limit_bytes=60 << 20),

time: 55.1 us -> 55.8 us (1.013)
  Pallas kernels: 54.9 us -> 55.6 us
    pallas_call x1, Pallas kernels: 1.53 us -> 2.36 us  [on_device(): pl.pallas_call(last_kernel, out_shape=jax.ShapeDtypeStruct((TS, K), F32),...]
where the time goes in v9:
time: 55.8 us; the launch traced here: 55.6 us
  Pallas kernels  55.6 us (100%)
    pallas_call x1, Pallas kernels, on_device(): pl.pallas_call(functools.partial(main_kernel, NX, NY, NZ, NC), out_shape=...  53.2 us
    pallas_call x1, Pallas kernels, on_device(): pl.pallas_call(last_kernel, out_shape=jax.ShapeDtypeStruct((TS, K), F32),...  2.36 us

profile of v9, /device:TPU:1, one launch (start us, length us, event | category | flops | bytes accessed | tf_op | source)
XLA Modules:
  0.0 55.6 jit_solution(12004188021313936828)
XLA Ops:
  0.0 53.2 %shard_map.37 = (f32[40,256]{1,0:T(8,128)}, f32[40,256]{1,0:T(8,128)}, f32[256,256]{1,0:T(8,128)}, f32[8,128]{1,0:T(8,128)}) custom-call(bf16[640,2560]{1,0:T(8,128)(2,1)} %depth_hbm.1, bf16[2560,256]{1,0:T(8,128)(2,1)} %gauss_hbm.1, s32[2560]{0:T(1024)} %keep_ref.1), custom_call_target="tpu_custom_call" | custom-call | tf_op jit(solution)/shard_map/pallas_call | solution.py:561
  53.3 2.4 %shard_map.38 = f32[40,256]{1,0:T(8,128)} custom-call(f32[40,256]{1,0:T(8,128)} %get-tuple-element.9.found_hbm, f32[8,128]{1,0:T(8,128)} %get-tuple-element.10.off_hbm, f32[40,256]{1,0:T(8,128)} %get-tuple-element.11.part_hbm, f32[256,256]{1,0:T(8,128)} %get-tuple-element.12.gram_hbm), custom_call_target="tpu_custom_call" | custom-call | tf_op jit(solution)/shard_map/pallas_call | solution.py:618
